TPU v7x, 256 devices: a whole 4x4x8 slice. The times are simulated.
256 devices in a mesh: depth: 4 (over x), slab: 64 (over y, z, core).
Axes of the slice: x: 4, y: 4, z: 8, core: 2. Of those that a mesh axis runs over, the one named last changes fastest.
Arguments:
- incident: bfloat16 [2, 2, 1536, 1536], P(None, None, 'slab'), may hold values from -6 to 6
- transmission: bfloat16 [4, 2, 1536, 1536], P('depth', None, 'slab'), may hold values from -4.1875 to 4.1875
- prop_phase: float32 [1536, 1536], P(None, 'slab'), may hold values from -3.140625 to 3.140625
- cotangent: bfloat16 [2, 2, 1536, 1536], P(None, None, 'slab'), may hold values from -6 to 6
Outputs:
- trans_grad: float32 [4, 2, 1536, 1536], P('depth', None, 'slab')
All inputs are finite; a program needn't handle non-finite values.
Results may differ from a plain program's by a relative error of at most 0.038.
Values may be sent and summed in bfloat16 or wider, within the bound.
A program may use at most 128 MiB of HBM per device.

v0:
```python
import math

import jax
import jax.numpy as jnp
from jax import lax
from jax.sharding import PartitionSpec as P


def from_behind(block, axis, distance):
    devices = range(lax.axis_size(axis))
    route = [(i - distance, i) for i in devices if i - distance in devices]
    return lax.ppermute(block, axis, route)


def make_tables(length):
    big_len = min(length, 512)
    small_len = length // big_len
    counter = jnp.arange(big_len, dtype=jnp.int32)
    product = counter[:, None] * counter[None, :] % big_len
    angles = product.astype(jnp.float32) * (2.0 * math.pi / big_len)
    big_cos = jnp.cos(angles).astype(jnp.bfloat16)
    big_sin = jnp.sin(angles).astype(jnp.bfloat16)
    little = jnp.arange(small_len, dtype=jnp.int32)
    twist_idx = counter[:, None] * little[None, :] % length
    twist_angles = twist_idx.astype(jnp.float32) * (2.0 * math.pi / length)
    small_idx = little[:, None] * little[None, :] % small_len
    small_angles = small_idx.astype(jnp.float32) * (2.0 * math.pi / small_len)
    return (
        big_cos,
        big_sin,
        jnp.cos(twist_angles),
        jnp.sin(twist_angles),
        jnp.cos(small_angles),
        jnp.sin(small_angles),
    )


def combine_parts(first_prod, second_prod, orient):
    real_part = first_prod[:, 0] + orient * second_prod[:, 1]
    imag_part = first_prod[:, 1] - orient * second_prod[:, 0]
    return jnp.stack([real_part, imag_part], axis=1)


def twisted(segment, twist_cos, twist_sin, orient):
    real_part = segment[:, 0] * twist_cos + orient * segment[:, 1] * twist_sin
    imag_part = segment[:, 1] * twist_cos - orient * segment[:, 0] * twist_sin
    return jnp.stack([real_part, imag_part], axis=1)


def along_columns(field, tables, orient):
    big_cos, big_sin, twist_cos, twist_sin, small_cos, small_sin = tables
    big_len = big_cos.shape[0]
    small_len = small_cos.shape[0]
    shaped = field.reshape(field.shape[:3] + (big_len, small_len))
    first_prod = jnp.einsum("mzrna,nk->mzrka", shaped, big_cos, preferred_element_type=jnp.float32)
    second_prod = jnp.einsum("mzrna,nk->mzrka", shaped, big_sin, preferred_element_type=jnp.float32)
    segment = twisted(combine_parts(first_prod, second_prod, orient), twist_cos, twist_sin, orient)
    first_prod = jnp.einsum("mzrka,aj->mzrjk", segment, small_cos, precision=lax.Precision.HIGHEST)
    second_prod = jnp.einsum("mzrka,aj->mzrjk", segment, small_sin, precision=lax.Precision.HIGHEST)
    return combine_parts(first_prod, second_prod, orient).reshape(field.shape)


def along_rows(field, tables, orient):
    big_cos, big_sin, twist_cos, twist_sin, small_cos, small_sin = tables
    big_len = big_cos.shape[0]
    small_len = small_cos.shape[0]
    shaped = field.reshape(field.shape[:2] + (big_len, small_len, field.shape[3]))
    first_prod = jnp.einsum("mznac,nk->mzkac", shaped, big_cos, preferred_element_type=jnp.float32)
    second_prod = jnp.einsum("mznac,nk->mzkac", shaped, big_sin, preferred_element_type=jnp.float32)
    segment = twisted(
        combine_parts(first_prod, second_prod, orient),
        twist_cos[:, :, None],
        twist_sin[:, :, None],
        orient,
    )
    first_prod = jnp.einsum("mzkac,aj->mzjkc", segment, small_cos, precision=lax.Precision.HIGHEST)
    second_prod = jnp.einsum("mzkac,aj->mzjkc", segment, small_sin, precision=lax.Precision.HIGHEST)
    return combine_parts(first_prod, second_prod, orient).reshape(field.shape)


def propagate(field, tables, kern_cos, kern_sin, is_valid):
    length = field.shape[3]

    def forward_rows(block_in):
        return along_columns(block_in, tables, 1.0).astype(jnp.bfloat16)

    def inverse_rows(block_in):
        return (along_columns(block_in, tables, -1.0) / length).astype(jnp.bfloat16)

    def spectral(block_in):
        spectrum = along_rows(block_in, tables, 1.0)
        real_part = spectrum[:, 0] * kern_cos - spectrum[:, 1] * kern_sin
        imag_part = spectrum[:, 1] * kern_cos + spectrum[:, 0] * kern_sin
        turned = jnp.stack([real_part, imag_part], axis=1).astype(jnp.bfloat16)
        return (along_rows(turned, tables, -1.0) / length).astype(jnp.bfloat16)

    spectrum_rows = lax.cond(is_valid, forward_rows, jnp.zeros_like, field)
    filtered = lax.cond(
        is_valid,
        spectral,
        jnp.zeros_like,
        lax.all_to_all(spectrum_rows, "slab", split_axis=3, concat_axis=2, tiled=True),
    )
    row_field = lax.all_to_all(filtered, "slab", split_axis=2, concat_axis=3, tiled=True)
    return lax.cond(is_valid, inverse_rows, jnp.zeros_like, row_field)


def transmit(field, trans_block):
    field_re = field[:, 0].astype(jnp.float32)
    field_im = field[:, 1].astype(jnp.float32)
    trans_re = trans_block[0].astype(jnp.float32)
    trans_im = trans_block[1].astype(jnp.float32)
    real_part = field_re * trans_re - field_im * trans_im
    imag_part = field_re * trans_im + field_im * trans_re
    return jnp.stack([real_part, imag_part], axis=1).astype(jnp.bfloat16)


def conj_product(left_field, right_field):
    left_re = left_field[:, 0].astype(jnp.float32)
    left_im = left_field[:, 1].astype(jnp.float32)
    right_re = right_field[:, 0].astype(jnp.float32)
    right_im = right_field[:, 1].astype(jnp.float32)
    real_part = left_re * right_re + left_im * right_im
    imag_part = left_re * right_im - left_im * right_re
    return jnp.stack([real_part, imag_part], axis=1)


def on_device(incident, transmission, prop_phase, cotangent):
    micro_total = incident.shape[0]
    slices_here = transmission.shape[0]
    length = incident.shape[3]
    depth_count = lax.axis_size("depth")
    segment_index = lax.axis_index("depth")
    tables = make_tables(length)
    kern_cos = jnp.cos(prop_phase)
    kern_sin = jnp.sin(prop_phase)
    group_size = 1
    blocks = micro_total // group_size
    turns = depth_count + blocks - 1
    field_shape = (group_size,) + incident.shape[1:]
    stash = jnp.zeros((slices_here, micro_total) + incident.shape[1:], jnp.bfloat16)
    carried = jnp.zeros(field_shape, jnp.bfloat16)
    for turn_num in range(turns):
        block_idx = turn_num - segment_index
        is_valid = (block_idx >= 0) & (block_idx < blocks)
        offset = jnp.clip(block_idx, 0, blocks - 1) * group_size
        fresh = lax.dynamic_slice_in_dim(incident, offset, group_size, 0)
        current = jnp.where(segment_index == 0, fresh, carried)
        slice_idx = 0
        entries = [current]
        current = propagate(
            transmit(current, transmission[slice_idx]), tables, kern_cos, kern_sin, is_valid
        )
        updated = lax.dynamic_update_slice_in_dim(stash, jnp.stack(entries, axis=0), offset, 1)
        stash = jnp.where(is_valid, updated, stash)
        carried = from_behind(current, "depth", 1)
    grads = [jnp.zeros(transmission.shape[1:], jnp.float32)]
    carried = jnp.zeros(field_shape, jnp.bfloat16)
    for turn_num in range(turns):
        block_idx = turn_num - (depth_count - 1 - segment_index)
        is_valid = (block_idx >= 0) & (block_idx < blocks)
        offset = jnp.clip(block_idx, 0, blocks - 1) * group_size
        fresh = lax.dynamic_slice_in_dim(cotangent, offset, group_size, 0)
        current = jnp.where(segment_index == depth_count - 1, fresh, carried)
        stored = lax.dynamic_slice_in_dim(stash, offset, group_size, 1)
        for slice_idx in reversed(range(slices_here)):
            pulled = propagate(current, tables, kern_cos, -kern_sin, is_valid)
            grads[slice_idx] = grads[slice_idx] + jnp.sum(
                conj_product(stored[slice_idx], pulled), axis=0
            )
            current = conj_product(transmission[slice_idx][None], pulled).astype(jnp.bfloat16)
        carried = from_behind(current, "depth", -1)
    return jnp.stack(grads, axis=0)


def solution(mesh):
    in_specs = (
        P(None, None, "slab", None),
        P("depth", None, "slab", None),
        P(None, "slab"),
        P(None, None, "slab", None),
    )
    out_specs = P("depth", None, "slab", None)
    return jax.shard_map(
        on_device, mesh=mesh, in_specs=in_specs, out_specs=out_specs, check_vma=False
    )
```

profile of v0, /device:TPU:1, one launch (start us, length us, event | category | flops | bytes accessed | tf_op | source)
XLA Modules:
  0.0 620.5 jit_solution(3319320029923208925)
XLA Ops:
  0.0 4.3 sine_convert_fusion
  6.9 13.2 %all-to-all-start.8 = ((bf16[64,2,576]{2,1,0:T(2,128)(2,1)}), bf16[64,2,576]{2,1,0:T(2,128)(2,1)S(1)}, u32[]{:S(2)}, u32[]{:S(2)}) async-start(bf16[64,2,576]{2,1,0:T(2,128)(2,1)} %reshape.4086), calls=%async_computation.8 | async-start | bytes 327680 | tf_op jit(solution)/shard_map/all_to_all | solution.py:102
  20.6 10.0 %all-to-all-done.8 = bf16[64,2,576]{2,1,0:T(2,128)(2,1)S(1)} async-done(((bf16[64,2,576]{2,1,0:T(2,128)(2,1)}), bf16[64,2,576]{2,1,0:T(2,128)(2,1)S(1)}, u32[]{:S(2)}, u32[]{:S(2)}) %all-to-all-start.8) | async-done | bytes 147488 | tf_op jit(solution)/shard_map/all_to_all | solution.py:102
  35.2 5.3 all-to-all-start.9
  41.3 9.8 %all-to-all-done.9 = bf16[64,2,576]{2,1,0:T(2,128)(2,1)S(1)} async-done(((bf16[64,2,576]{2,1,0:T(2,128)(2,1)}), bf16[64,2,576]{2,1,0:T(2,128)(2,1)S(1)}, u32[]{:S(2)}, u32[]{:S(2)}) %all-to-all-start.9) | async-done | bytes 147488 | tf_op jit(solution)/shard_map/all_to_all | solution.py:104
  55.8 4.4 conditional.27
  62.5 5.3 all-to-all-start
  67.9 10.6 %all-to-all-done = bf16[64,2,576]{2,1,0:T(2,128)(2,1)S(1)} async-done(((bf16[64,2,576]{2,1,0:T(2,128)(2,1)}), bf16[64,2,576]{2,1,0:T(2,128)(2,1)S(1)}, u32[]{:S(2)}, u32[]{:S(2)}) %all-to-all-start) | async-done | bytes 147488 | tf_op jit(solution)/shard_map/all_to_all | solution.py:102
  80.5 10.0 %conditional.28 = (bf16[1,2,1536,24]{2,3,1,0:T(8,128)(2,1)}) conditional(s32[]{:T(128)} %convert_element_type.1530, () %tuple.178, (bf16[1,2,64,24,24]{4,2,3,1,0:T(8,128)(2,1)S(1)}, bf16[512,512]{1,0:T(8,128)(2,1)S(1)}, bf16[512,512]{1,0:T(8,128)(2,1)S(1)}, f32[512,3]{0,1:T(4,128)S(1)}, f32[512,3]{0,1:T(4,128)S(1)}, ...), branch_computations={%region_2.3_spmd, %region_3.4_spmd} | conditional | flops 314305536 | bytes 14852248 | solution.py:98
  94.3 5.5 all-to-all-start.1
  101.2 5.6 collective-permute-done.4
  111.3 11.4 %all-to-all-start.10 = ((bf16[64,2,576]{2,1,0:T(2,128)(2,1)}), bf16[64,2,576]{2,1,0:T(2,128)(2,1)}, u32[]{:S(2)}, u32[]{:S(2)}) async-start(bf16[64,2,576]{2,1,0:T(2,128)(2,1)} %reshape.4090), calls=%async_computation.10 | async-start | bytes 327680 | tf_op jit(solution)/shard_map/all_to_all | solution.py:102
  122.7 2.6 reshape.4073
  127.8 7.4 %conditional.29 = (bf16[1,2,24,1536]{3,2,1,0:T(8,128)(2,1)}) conditional(s32[]{:T(128)} %convert_element_type.1530, () %tuple.177, (bf16[1,2,24,64,24]{2,3,4,1,0:T(8,128)(2,1)S(1)}, bf16[512,512]{1,0:T(8,128)(2,1)S(1)}, bf16[512,512]{1,0:T(8,128)(2,1)S(1)}, f32[512,3]{0,1:T(4,128)S(1)}, f32[512,3]{0,1:T(4,128)S(1)}, ...), branch_computations={%region_4.5_spmd, %region_5.6_spmd} | conditional | flops 157117440 | bytes 7143504 | solution.py:105
  147.0 10.3 %all-to-all-start.11 = ((bf16[64,2,576]{2,1,0:T(2,128)(2,1)}), bf16[64,2,576]{2,1,0:T(2,128)(2,1)S(1)}, u32[]{:S(2)}, u32[]{:S(2)}) async-start(bf16[64,2,576]{2,1,0:T(2,128)(2,1)} %reshape.4092), calls=%async_computation.11 | async-start | bytes 327680 | tf_op jit(solution)/shard_map/all_to_all | solution.py:104
  158.1 9.8 %all-to-all-done.11 = bf16[64,2,576]{2,1,0:T(2,128)(2,1)S(1)} async-done(((bf16[64,2,576]{2,1,0:T(2,128)(2,1)}), bf16[64,2,576]{2,1,0:T(2,128)(2,1)S(1)}, u32[]{:S(2)}, u32[]{:S(2)}) %all-to-all-start.11) | async-done | bytes 147488 | tf_op jit(solution)/shard_map/all_to_all | solution.py:104
  175.0 8.5 %conditional.30 = (bf16[1,2,24,1536]{3,2,1,0:T(8,128)(2,1)S(1)}) conditional(s32[]{:T(128)} %convert_element_type.1540, () %tuple.185, (bf16[1,2,24,1536]{3,2,1,0:T(8,128)(2,1)}, bf16[512,512]{1,0:T(8,128)(2,1)S(1)}, bf16[512,512]{1,0:T(8,128)(2,1)S(1)}, f32[512,3]{0,1:T(4,128)S(1)}, f32[512,3]{0,1:T(4,128)S(1)}, /*index=5*/f32[512,3]{0,1:T(4,128)S(1)}, ...), branch_computations={%region_6.7_spmd, %region_7.8_spmd} | conditional | flops 156893184 | bytes 6529104 | solution.py:97
  187.9 5.5 all-to-all-start.2
  194.8 20.6 %collective-permute-done.5 = bf16[1,2,24,1536]{3,2,1,0:T(8,128)(2,1)S(1)} collective-permute-done((bf16[1,2,24,1536]{3,2,1,0:T(8,128)(2,1)S(1)}, bf16[1,2,24,1536]{3,2,1,0:T(8,128)(2,1)S(1)}, u32[]{:S(2)}, u32[]{:S(2)}) %collective-permute-start.5) | collective-permute-done | bytes 147488 | tf_op jit(solution)/shard_map/ppermute | solution.py:12
  217.9 11.2 %all-to-all-start.12 = ((bf16[64,2,576]{2,1,0:T(2,128)(2,1)}), bf16[64,2,576]{2,1,0:T(2,128)(2,1)}, u32[]{:S(2)}, u32[]{:S(2)}) async-start(bf16[64,2,576]{2,1,0:T(2,128)(2,1)} %reshape.4094), calls=%async_computation.12 | async-start | bytes 327680 | tf_op jit(solution)/shard_map/all_to_all | solution.py:102
  234.2 16.5 %conditional.31 = (bf16[1,2,1536,24]{2,3,1,0:T(8,128)(2,1)S(1)}) conditional(s32[]{:T(128)} %convert_element_type.1540, () %tuple.184, (bf16[1,2,64,24,24]{4,2,3,1,0:T(8,128)(2,1)S(1)}, bf16[512,512]{1,0:T(8,128)(2,1)S(1)}, bf16[512,512]{1,0:T(8,128)(2,1)S(1)}, f32[512,3]{0,1:T(4,128)S(1)}, f32[512,3]{0,1:T(4,128)S(1)}, ...), branch_computations={%region_8.9_spmd, %region_9.10_spmd} | conditional | flops 314305536 | bytes 14852248 | solution.py:98
  253.1 10.5 %all-to-all-start.3 = ((bf16[64,2,576]{2,1,0:T(2,128)(2,1)}), bf16[64,2,576]{2,1,0:T(2,128)(2,1)}, u32[]{:S(2)}, u32[]{:S(2)}) async-start(bf16[64,2,576]{2,1,0:T(2,128)(2,1)} %reshape.4076), calls=%async_computation.3 | async-start | bytes 327680 | tf_op jit(solution)/shard_map/all_to_all | solution.py:104
  271.5 2.6 all-to-all-done.3
  274.1 7.9 %all-to-all-start.13 = ((bf16[64,2,576]{2,1,0:T(2,128)(2,1)}), bf16[64,2,576]{2,1,0:T(2,128)(2,1)}, u32[]{:S(2)}, u32[]{:S(2)}) async-start(bf16[64,2,576]{2,1,0:T(2,128)(2,1)} %reshape.4096), calls=%async_computation.13 | async-start | bytes 327680 | tf_op jit(solution)/shard_map/all_to_all | solution.py:104
  287.1 9.2 %conditional.32 = (bf16[1,2,24,1536]{3,2,1,0:T(8,128)(2,1)}) conditional(s32[]{:T(128)} %convert_element_type.1540, () %tuple.183, (bf16[1,2,24,64,24]{2,3,4,1,0:T(8,128)(2,1)S(1)}, bf16[512,512]{1,0:T(8,128)(2,1)S(1)}, bf16[512,512]{1,0:T(8,128)(2,1)S(1)}, f32[512,3]{0,1:T(4,128)S(1)}, f32[512,3]{0,1:T(4,128)S(1)}, ...), branch_computations={%region_10.11_spmd, %region_11.12_spmd} | conditional | flops 157117440 | bytes 7143504 | solution.py:105
  296.3 39.8 %collective-permute-start.1 = (bf16[1,2,24,1536]{3,2,1,0:T(8,128)(2,1)}, bf16[1,2,24,1536]{3,2,1,0:T(8,128)(2,1)}, u32[]{:S(2)}, u32[]{:S(2)}) collective-permute-start(bf16[1,2,24,1536]{3,2,1,0:T(8,128)(2,1)} %get-tuple-element.2096), channel_id=1, source_target_pairs={{0,64},{64,128},{128,192},{1,65},{65,129},{129,193},{2,66},{66,130... | collective-permute-start | bytes 442376 | tf_op jit(solution)/shard_map/ppermute | solution.py:12
  347.4 10.8 %all-to-all-start.4 = ((bf16[64,2,576]{2,1,0:T(2,128)(2,1)}), bf16[64,2,576]{2,1,0:T(2,128)(2,1)}, u32[]{:S(2)}, u32[]{:S(2)}) async-start(bf16[64,2,576]{2,1,0:T(2,128)(2,1)} %reshape.4078), calls=%async_computation.4 | async-start | bytes 327680 | tf_op jit(solution)/shard_map/all_to_all | solution.py:102
  359.6 21.2 %collective-permute-done.6 = bf16[1,2,24,1536]{3,2,1,0:T(8,128)(2,1)S(1)} collective-permute-done((bf16[1,2,24,1536]{3,2,1,0:T(8,128)(2,1)S(1)}, bf16[1,2,24,1536]{3,2,1,0:T(8,128)(2,1)S(1)}, u32[]{:S(2)}, u32[]{:S(2)}) %collective-permute-start.6) | collective-permute-done | bytes 147488 | tf_op jit(solution)/shard_map/ppermute | solution.py:12
  380.7 10.4 %conditional.48 = (bf16[1,2,24,1536]{3,2,1,0:T(8,128)(2,1)S(1)}) conditional(s32[]{:T(128)} %convert_element_type.1565, () %tuple.221, (pred[]{:T(512)}, bf16[2,2,24,1536]{3,2,1,0:T(8,128)(2,1)S(1)}, s32[]{:T(128)}, bf16[1,2,24,1536]{3,2,1,0:T(8,128)(2,1)S(1)}, bf16[512,512]{1,0:T(8,128)(2,1)S(1)}, /*index=5*/bf16[512,512]{1,0:T(8,128)(2,1)S(1)}, ...), branch_computations={%region_42.43_spmd, %region_43.44_spmd} | conditional | flops 156966912 | bytes 7561301 | solution.py:97
  380.7 2.8 copy.503
  393.4 11.2 %all-to-all-start.14 = ((bf16[64,2,576]{2,1,0:T(2,128)(2,1)}), bf16[64,2,576]{2,1,0:T(2,128)(2,1)}, u32[]{:S(2)}, u32[]{:S(2)}) async-start(bf16[64,2,576]{2,1,0:T(2,128)(2,1)} %reshape.4098), calls=%async_computation.14 | async-start | bytes 327680 | tf_op jit(solution)/shard_map/all_to_all | solution.py:102
  412.5 2.6 all-to-all-done.14
  415.1 7.8 %all-to-all-start.5 = ((bf16[64,2,576]{2,1,0:T(2,128)(2,1)}), bf16[64,2,576]{2,1,0:T(2,128)(2,1)}, u32[]{:S(2)}, u32[]{:S(2)}) async-start(bf16[64,2,576]{2,1,0:T(2,128)(2,1)} %reshape.4080), calls=%async_computation.5 | async-start | bytes 327680 | tf_op jit(solution)/shard_map/all_to_all | solution.py:104
  428.1 16.5 %conditional.49 = (bf16[1,2,1536,24]{2,3,1,0:T(8,128)(2,1)S(1)}) conditional(s32[]{:T(128)} %convert_element_type.1565, () %tuple.220, (bf16[1,2,64,24,24]{4,2,3,1,0:T(8,128)(2,1)S(1)}, bf16[512,512]{1,0:T(8,128)(2,1)S(1)}, bf16[512,512]{1,0:T(8,128)(2,1)S(1)}, f32[512,3]{0,1:T(4,128)S(1)}, f32[512,3]{0,1:T(4,128)S(1)}, ...), branch_computations={%region_44.45_spmd, %region_45.46_spmd} | conditional | flops 314305536 | bytes 14852248 | solution.py:98
  446.9 10.5 %all-to-all-start.15 = ((bf16[64,2,576]{2,1,0:T(2,128)(2,1)}), bf16[64,2,576]{2,1,0:T(2,128)(2,1)}, u32[]{:S(2)}, u32[]{:S(2)}) async-start(bf16[64,2,576]{2,1,0:T(2,128)(2,1)} %reshape.4100), calls=%async_computation.15 | async-start | bytes 327680 | tf_op jit(solution)/shard_map/all_to_all | solution.py:104
  463.4 28.7 %collective-permute-start.2 = (bf16[1,2,24,1536]{3,2,1,0:T(8,128)(2,1)}, bf16[1,2,24,1536]{3,2,1,0:T(8,128)(2,1)}, u32[]{:S(2)}, u32[]{:S(2)}) collective-permute-start(bf16[1,2,24,1536]{3,2,1,0:T(8,128)(2,1)} %get-tuple-element.2099), channel_id=1, source_target_pairs={{0,64},{64,128},{128,192},{1,65},{65,129},{129,193},{2,66},{66,130... | collective-permute-start | bytes 442376 | tf_op jit(solution)/shard_map/ppermute | solution.py:12
  497.3 8.4 %conditional.50 = (bf16[1,2,24,1536]{3,2,1,0:T(8,128)(2,1)S(1)}) conditional(s32[]{:T(128)} %convert_element_type.1565, () %tuple.219, (bf16[1,2,24,64,24]{2,3,4,1,0:T(8,128)(2,1)S(1)}, bf16[512,512]{1,0:T(8,128)(2,1)S(1)}, bf16[512,512]{1,0:T(8,128)(2,1)S(1)}, f32[512,3]{0,1:T(4,128)S(1)}, f32[512,3]{0,1:T(4,128)S(1)}, ...), branch_computations={%region_46.47_spmd, %region_47.48_spmd} | conditional | flops 157117440 | bytes 7143504 | solution.py:105
  509.3 10.6 %all-to-all-start.6 = ((bf16[64,2,576]{2,1,0:T(2,128)(2,1)}), bf16[64,2,576]{2,1,0:T(2,128)(2,1)S(1)}, u32[]{:S(2)}, u32[]{:S(2)}) async-start(bf16[64,2,576]{2,1,0:T(2,128)(2,1)} %reshape.4082), calls=%async_computation.6 | async-start | bytes 327680 | tf_op jit(solution)/shard_map/all_to_all | solution.py:102
  521.3 5.6 collective-permute-done.7
  526.9 9.1 %conditional.51 = (bf16[1,2,24,1536]{3,2,1,0:T(8,128)(2,1)S(1)}) conditional(s32[]{:T(128)} %convert_element_type.1570, () %tuple.227, (pred[]{:T(512)}, bf16[2,2,24,1536]{3,2,1,0:T(8,128)(2,1)S(1)}, s32[]{:T(128)}, bf16[1,2,24,1536]{3,2,1,0:T(8,128)(2,1)S(1)}, bf16[512,512]{1,0:T(8,128)(2,1)S(1)}, /*index=5*/bf16[512,512]{1,0:T(8,128)(2,1)S(1)}, ...), branch_computations={%region_48.49_spmd, %region_49.50_spmd} | conditional | flops 156966912 | bytes 7561301 | solution.py:97
  526.9 2.8 copy.511
  540.9 11.3 %all-to-all-start.16 = ((bf16[64,2,576]{2,1,0:T(2,128)(2,1)}), bf16[64,2,576]{2,1,0:T(2,128)(2,1)S(1)}, u32[]{:S(2)}, u32[]{:S(2)}) async-start(bf16[64,2,576]{2,1,0:T(2,128)(2,1)} %reshape.4102), calls=%async_computation.16 | async-start | bytes 327680 | tf_op jit(solution)/shard_map/all_to_all | solution.py:102
  557.7 5.1 all-to-all-done.16
  563.4 5.3 all-to-all-start.7
  571.8 9.1 %conditional.52 = (bf16[1,2,1536,24]{2,3,1,0:T(8,128)(2,1)S(1)}) conditional(s32[]{:T(128)} %convert_element_type.1570, () %tuple.226, (bf16[1,2,64,24,24]{4,2,3,1,0:T(8,128)(2,1)S(1)}, bf16[512,512]{1,0:T(8,128)(2,1)S(1)}, bf16[512,512]{1,0:T(8,128)(2,1)S(1)}, f32[512,3]{0,1:T(4,128)S(1)}, f32[512,3]{0,1:T(4,128)S(1)}, ...), branch_computations={%region_50.51_spmd, %region_51.52_spmd} | conditional | flops 314305536 | bytes 14852248 | solution.py:98
  583.2 10.5 %all-to-all-start.17 = ((bf16[64,2,576]{2,1,0:T(2,128)(2,1)}), bf16[64,2,576]{2,1,0:T(2,128)(2,1)}, u32[]{:S(2)}, u32[]{:S(2)}) async-start(bf16[64,2,576]{2,1,0:T(2,128)(2,1)} %reshape.4104), calls=%async_computation.17 | async-start | bytes 327680 | tf_op jit(solution)/shard_map/all_to_all | solution.py:104
  598.2 6.1 all-to-all-done.17
  611.7 4.7 conditional.53
  (435 shorter events, 263.0 us)
Async XLA Ops:
  4.5 15.5 %copy-start.31 = (f32[1536,24]{0,1:T(8,128)S(1)}, f32[1536,24]{0,1:T(8,128)}, u32[]{:S(2)}) copy-start(f32[1536,24]{0,1:T(8,128)} %param.60) | copy-start | bytes 442372
  6.9 23.8 %all-to-all-start.8 = ((bf16[64,2,576]{2,1,0:T(2,128)(2,1)}), bf16[64,2,576]{2,1,0:T(2,128)(2,1)S(1)}, u32[]{:S(2)}, u32[]{:S(2)}) async-start(bf16[64,2,576]{2,1,0:T(2,128)(2,1)} %reshape.4086), calls=%async_computation.8 | async-start | bytes 327680 | tf_op jit(solution)/shard_map/all_to_all | solution.py:102
  32.9 7.7 %copy-start.2 = (bf16[2,2,24,1536]{3,2,1,0:T(8,128)(2,1)S(1)}, bf16[2,2,24,1536]{3,2,1,0:T(8,128)(2,1)}, u32[]{:S(2)}) copy-start(bf16[2,2,24,1536]{3,2,1,0:T(8,128)(2,1)} %param.58) | copy-start | bytes 884740
  35.2 15.9 %all-to-all-start.9 = ((bf16[64,2,576]{2,1,0:T(2,128)(2,1)}), bf16[64,2,576]{2,1,0:T(2,128)(2,1)S(1)}, u32[]{:S(2)}, u32[]{:S(2)}) async-start(bf16[64,2,576]{2,1,0:T(2,128)(2,1)} %reshape.4088), calls=%async_computation.9 | async-start | bytes 327680 | tf_op jit(solution)/shard_map/all_to_all | solution.py:104
  53.5 2.3 copy-start.5
  62.5 15.9 %all-to-all-start = ((bf16[64,2,576]{2,1,0:T(2,128)(2,1)}), bf16[64,2,576]{2,1,0:T(2,128)(2,1)S(1)}, u32[]{:S(2)}, u32[]{:S(2)}) async-start(bf16[64,2,576]{2,1,0:T(2,128)(2,1)} %reshape.4070), calls=%async_computation | async-start | bytes 327680 | tf_op jit(solution)/shard_map/all_to_all | solution.py:102
  90.5 9.3 %copy-start.23 = (bf16[1,1,24,1536]{3,2,1,0:T(8,128)(2,1)S(1)}, bf16[1,1,24,1536]{3,2,1,0:T(8,128)(2,1)}, u32[]{:S(2)}) copy-start(bf16[1,1,24,1536]{3,2,1,0:T(8,128)(2,1)} %get-tuple-element.2063) | copy-start | bytes 221188
  90.5 9.3 %copy-start.24 = (bf16[1,1,24,1536]{3,2,1,0:T(8,128)(2,1)S(1)}, bf16[1,1,24,1536]{3,2,1,0:T(8,128)(2,1)}, u32[]{:S(2)}) copy-start(bf16[1,1,24,1536]{3,2,1,0:T(8,128)(2,1)} %get-tuple-element.2064) | copy-start | bytes 221188
  90.5 16.2 %copy-start = (bf16[2,2,24,1536]{3,2,1,0:T(8,128)(2,1)S(1)}, bf16[2,2,24,1536]{3,2,1,0:T(8,128)(2,1)}, u32[]{:S(2)}) copy-start(bf16[2,2,24,1536]{3,2,1,0:T(8,128)(2,1)} %param.61) | copy-start | bytes 884740
  94.3 17.0 %all-to-all-start.1 = ((bf16[64,2,576]{2,1,0:T(2,128)(2,1)}), bf16[64,2,576]{2,1,0:T(2,128)(2,1)}, u32[]{:S(2)}, u32[]{:S(2)}) async-start(bf16[64,2,576]{2,1,0:T(2,128)(2,1)} %reshape.4072), calls=%async_computation.1 | async-start | bytes 327680 | tf_op jit(solution)/shard_map/all_to_all | solution.py:104
  99.9 6.9 %collective-permute-start.4 = (bf16[1,2,24,1536]{3,2,1,0:T(8,128)(2,1)S(1)}, bf16[1,2,24,1536]{3,2,1,0:T(8,128)(2,1)S(1)}, u32[]{:S(2)}, u32[]{:S(2)}) collective-permute-start(bf16[1,2,24,1536]{3,2,1,0:T(8,128)(2,1)S(1)} %pad_maximum_fusion.40), channel_id=1, source_target_pairs={{64,0},{128,64},{192,128},{65,1},{129,65},{193,129},{66,2},{130,66... | collective-permute-start | bytes 442376 | tf_op jit(solution)/shard_map/ppermute | solution.py:12
  111.3 25.9 %all-to-all-start.10 = ((bf16[64,2,576]{2,1,0:T(2,128)(2,1)}), bf16[64,2,576]{2,1,0:T(2,128)(2,1)}, u32[]{:S(2)}, u32[]{:S(2)}) async-start(bf16[64,2,576]{2,1,0:T(2,128)(2,1)} %reshape.4090), calls=%async_computation.10 | async-start | bytes 327680 | tf_op jit(solution)/shard_map/all_to_all | solution.py:102
  135.3 22.1 %collective-permute-start = (bf16[1,2,24,1536]{3,2,1,0:T(8,128)(2,1)}, bf16[1,2,24,1536]{3,2,1,0:T(8,128)(2,1)}, u32[]{:S(2)}, u32[]{:S(2)}) collective-permute-start(bf16[1,2,24,1536]{3,2,1,0:T(8,128)(2,1)} %get-tuple-element.2093), channel_id=1, source_target_pairs={{0,64},{64,128},{128,192},{1,65},{65,129},{129,193},{2,66},{66,130... | collective-permute-start | bytes 442376 | tf_op jit(solution)/shard_map/ppermute | solution.py:12
  143.3 14.1 %copy-start.3 = (bf16[2,2,24,1536]{3,2,1,0:T(8,128)(2,1)S(1)}, bf16[2,2,24,1536]{3,2,1,0:T(8,128)(2,1)}, u32[]{:S(2)}) copy-start(bf16[2,2,24,1536]{3,2,1,0:T(8,128)(2,1)} %param.58) | copy-start | bytes 884740
  147.0 20.9 %all-to-all-start.11 = ((bf16[64,2,576]{2,1,0:T(2,128)(2,1)}), bf16[64,2,576]{2,1,0:T(2,128)(2,1)S(1)}, u32[]{:S(2)}, u32[]{:S(2)}) async-start(bf16[64,2,576]{2,1,0:T(2,128)(2,1)} %reshape.4092), calls=%async_computation.11 | async-start | bytes 327680 | tf_op jit(solution)/shard_map/all_to_all | solution.py:104
  172.6 2.4 copy-start.7
  184.2 9.3 %copy-start.25 = (bf16[1,1,24,1536]{3,2,1,0:T(8,128)(2,1)S(1)}, bf16[1,1,24,1536]{3,2,1,0:T(8,128)(2,1)}, u32[]{:S(2)}) copy-start(bf16[1,1,24,1536]{3,2,1,0:T(8,128)(2,1)} %get-tuple-element.2059) | copy-start | bytes 221188
  184.2 9.3 %copy-start.26 = (bf16[1,1,24,1536]{3,2,1,0:T(8,128)(2,1)S(1)}, bf16[1,1,24,1536]{3,2,1,0:T(8,128)(2,1)}, u32[]{:S(2)}) copy-start(bf16[1,1,24,1536]{3,2,1,0:T(8,128)(2,1)} %get-tuple-element.2060) | copy-start | bytes 221188
  187.9 30.0 %all-to-all-start.2 = ((bf16[64,2,576]{2,1,0:T(2,128)(2,1)}), bf16[64,2,576]{2,1,0:T(2,128)(2,1)}, u32[]{:S(2)}, u32[]{:S(2)}) async-start(bf16[64,2,576]{2,1,0:T(2,128)(2,1)} %reshape.4074), calls=%async_computation.2 | async-start | bytes 327680 | tf_op jit(solution)/shard_map/all_to_all | solution.py:102
  193.5 21.9 %collective-permute-start.5 = (bf16[1,2,24,1536]{3,2,1,0:T(8,128)(2,1)S(1)}, bf16[1,2,24,1536]{3,2,1,0:T(8,128)(2,1)S(1)}, u32[]{:S(2)}, u32[]{:S(2)}) collective-permute-start(bf16[1,2,24,1536]{3,2,1,0:T(8,128)(2,1)S(1)} %pad_maximum_fusion.41), channel_id=1, source_target_pairs={{64,0},{128,64},{192,128},{65,1},{129,65},{193,129},{66,2},{130,66... | collective-permute-start | bytes 442376 | tf_op jit(solution)/shard_map/ppermute | solution.py:12
  217.9 35.2 %all-to-all-start.12 = ((bf16[64,2,576]{2,1,0:T(2,128)(2,1)}), bf16[64,2,576]{2,1,0:T(2,128)(2,1)}, u32[]{:S(2)}, u32[]{:S(2)}) async-start(bf16[64,2,576]{2,1,0:T(2,128)(2,1)} %reshape.4094), calls=%async_computation.12 | async-start | bytes 327680 | tf_op jit(solution)/shard_map/all_to_all | solution.py:102
  253.1 21.0 %all-to-all-start.3 = ((bf16[64,2,576]{2,1,0:T(2,128)(2,1)}), bf16[64,2,576]{2,1,0:T(2,128)(2,1)}, u32[]{:S(2)}, u32[]{:S(2)}) async-start(bf16[64,2,576]{2,1,0:T(2,128)(2,1)} %reshape.4076), calls=%async_computation.3 | async-start | bytes 327680 | tf_op jit(solution)/shard_map/all_to_all | solution.py:104
  274.1 62.0 %all-to-all-start.13 = ((bf16[64,2,576]{2,1,0:T(2,128)(2,1)}), bf16[64,2,576]{2,1,0:T(2,128)(2,1)}, u32[]{:S(2)}, u32[]{:S(2)}) async-start(bf16[64,2,576]{2,1,0:T(2,128)(2,1)} %reshape.4096), calls=%async_computation.13 | async-start | bytes 327680 | tf_op jit(solution)/shard_map/all_to_all | solution.py:104
  296.3 45.0 %collective-permute-start.1 = (bf16[1,2,24,1536]{3,2,1,0:T(8,128)(2,1)}, bf16[1,2,24,1536]{3,2,1,0:T(8,128)(2,1)}, u32[]{:S(2)}, u32[]{:S(2)}) collective-permute-start(bf16[1,2,24,1536]{3,2,1,0:T(8,128)(2,1)} %get-tuple-element.2096), channel_id=1, source_target_pairs={{0,64},{64,128},{128,192},{1,65},{65,129},{129,193},{2,66},{66,130... | collective-permute-start | bytes 442376 | tf_op jit(solution)/shard_map/ppermute | solution.py:12
  341.3 1.5 copy-start.9
  343.7 14.5 %copy-start.27 = (bf16[1,1,24,1536]{3,2,1,0:T(8,128)(2,1)S(1)}, bf16[1,1,24,1536]{3,2,1,0:T(8,128)(2,1)}, u32[]{:S(2)}) copy-start(bf16[1,1,24,1536]{3,2,1,0:T(8,128)(2,1)} %get-tuple-element.2055) | copy-start | bytes 221188
  343.7 14.5 %copy-start.28 = (bf16[1,1,24,1536]{3,2,1,0:T(8,128)(2,1)S(1)}, bf16[1,1,24,1536]{3,2,1,0:T(8,128)(2,1)}, u32[]{:S(2)}) copy-start(bf16[1,1,24,1536]{3,2,1,0:T(8,128)(2,1)} %get-tuple-element.2056) | copy-start | bytes 221188
  347.4 46.0 %all-to-all-start.4 = ((bf16[64,2,576]{2,1,0:T(2,128)(2,1)}), bf16[64,2,576]{2,1,0:T(2,128)(2,1)}, u32[]{:S(2)}, u32[]{:S(2)}) async-start(bf16[64,2,576]{2,1,0:T(2,128)(2,1)} %reshape.4078), calls=%async_computation.4 | async-start | bytes 327680 | tf_op jit(solution)/shard_map/all_to_all | solution.py:102
  358.3 22.5 %collective-permute-start.6 = (bf16[1,2,24,1536]{3,2,1,0:T(8,128)(2,1)S(1)}, bf16[1,2,24,1536]{3,2,1,0:T(8,128)(2,1)S(1)}, u32[]{:S(2)}, u32[]{:S(2)}) collective-permute-start(bf16[1,2,24,1536]{3,2,1,0:T(8,128)(2,1)S(1)} %pad_maximum_fusion.42), channel_id=1, source_target_pairs={{64,0},{128,64},{192,128},{65,1},{129,65},{193,129},{66,2},{130,66... | collective-permute-start | bytes 442376 | tf_op jit(solution)/shard_map/ppermute | solution.py:12
  393.4 21.7 %all-to-all-start.14 = ((bf16[64,2,576]{2,1,0:T(2,128)(2,1)}), bf16[64,2,576]{2,1,0:T(2,128)(2,1)}, u32[]{:S(2)}, u32[]{:S(2)}) async-start(bf16[64,2,576]{2,1,0:T(2,128)(2,1)} %reshape.4098), calls=%async_computation.14 | async-start | bytes 327680 | tf_op jit(solution)/shard_map/all_to_all | solution.py:102
  415.1 31.8 %all-to-all-start.5 = ((bf16[64,2,576]{2,1,0:T(2,128)(2,1)}), bf16[64,2,576]{2,1,0:T(2,128)(2,1)}, u32[]{:S(2)}, u32[]{:S(2)}) async-start(bf16[64,2,576]{2,1,0:T(2,128)(2,1)} %reshape.4080), calls=%async_computation.5 | async-start | bytes 327680 | tf_op jit(solution)/shard_map/all_to_all | solution.py:104
  446.9 45.2 %all-to-all-start.15 = ((bf16[64,2,576]{2,1,0:T(2,128)(2,1)}), bf16[64,2,576]{2,1,0:T(2,128)(2,1)}, u32[]{:S(2)}, u32[]{:S(2)}) async-start(bf16[64,2,576]{2,1,0:T(2,128)(2,1)} %reshape.4100), calls=%async_computation.15 | async-start | bytes 327680 | tf_op jit(solution)/shard_map/all_to_all | solution.py:104
  463.4 42.2 %collective-permute-start.2 = (bf16[1,2,24,1536]{3,2,1,0:T(8,128)(2,1)}, bf16[1,2,24,1536]{3,2,1,0:T(8,128)(2,1)}, u32[]{:S(2)}, u32[]{:S(2)}) collective-permute-start(bf16[1,2,24,1536]{3,2,1,0:T(8,128)(2,1)} %get-tuple-element.2099), channel_id=1, source_target_pairs={{0,64},{64,128},{128,192},{1,65},{65,129},{129,193},{2,66},{66,130... | collective-permute-start | bytes 442376 | tf_op jit(solution)/shard_map/ppermute | solution.py:12
  507.0 12.9 %copy-start.29 = (bf16[1,1,24,1536]{3,2,1,0:T(8,128)(2,1)S(1)}, bf16[1,1,24,1536]{3,2,1,0:T(8,128)(2,1)}, u32[]{:S(2)}) copy-start(bf16[1,1,24,1536]{3,2,1,0:T(8,128)(2,1)} %get-tuple-element.2051) | copy-start | bytes 221188
  507.0 12.9 %copy-start.30 = (bf16[1,1,24,1536]{3,2,1,0:T(8,128)(2,1)S(1)}, bf16[1,1,24,1536]{3,2,1,0:T(8,128)(2,1)}, u32[]{:S(2)}) copy-start(bf16[1,1,24,1536]{3,2,1,0:T(8,128)(2,1)} %get-tuple-element.2052) | copy-start | bytes 221188
  509.3 30.9 %all-to-all-start.6 = ((bf16[64,2,576]{2,1,0:T(2,128)(2,1)}), bf16[64,2,576]{2,1,0:T(2,128)(2,1)S(1)}, u32[]{:S(2)}, u32[]{:S(2)}) async-start(bf16[64,2,576]{2,1,0:T(2,128)(2,1)} %reshape.4082), calls=%async_computation.6 | async-start | bytes 327680 | tf_op jit(solution)/shard_map/all_to_all | solution.py:102
  520.0 6.9 %collective-permute-start.7 = (bf16[1,2,24,1536]{3,2,1,0:T(8,128)(2,1)S(1)}, bf16[1,2,24,1536]{3,2,1,0:T(8,128)(2,1)S(1)}, u32[]{:S(2)}, u32[]{:S(2)}) collective-permute-start(bf16[1,2,24,1536]{3,2,1,0:T(8,128)(2,1)S(1)} %pad_maximum_fusion.43), channel_id=1, source_target_pairs={{64,0},{128,64},{192,128},{65,1},{129,65},{193,129},{66,2},{130,66... | collective-permute-start | bytes 442376 | tf_op jit(solution)/shard_map/ppermute | solution.py:12
  540.9 21.9 %all-to-all-start.16 = ((bf16[64,2,576]{2,1,0:T(2,128)(2,1)}), bf16[64,2,576]{2,1,0:T(2,128)(2,1)S(1)}, u32[]{:S(2)}, u32[]{:S(2)}) async-start(bf16[64,2,576]{2,1,0:T(2,128)(2,1)} %reshape.4102), calls=%async_computation.16 | async-start | bytes 327680 | tf_op jit(solution)/shard_map/all_to_all | solution.py:102
  563.4 19.8 %all-to-all-start.7 = ((bf16[64,2,576]{2,1,0:T(2,128)(2,1)}), bf16[64,2,576]{2,1,0:T(2,128)(2,1)S(1)}, u32[]{:S(2)}, u32[]{:S(2)}) async-start(bf16[64,2,576]{2,1,0:T(2,128)(2,1)} %reshape.4084), calls=%async_computation.7 | async-start | bytes 327680 | tf_op jit(solution)/shard_map/all_to_all | solution.py:104
  583.2 21.0 %all-to-all-start.17 = ((bf16[64,2,576]{2,1,0:T(2,128)(2,1)}), bf16[64,2,576]{2,1,0:T(2,128)(2,1)}, u32[]{:S(2)}, u32[]{:S(2)}) async-start(bf16[64,2,576]{2,1,0:T(2,128)(2,1)} %reshape.4104), calls=%async_computation.17 | async-start | bytes 327680 | tf_op jit(solution)/shard_map/all_to_all | solution.py:104
  596.7 11.2 %copy-start.4 = (bf16[2,2,24,1536]{3,2,1,0:T(8,128)(2,1)S(1)}, bf16[2,2,24,1536]{3,2,1,0:T(8,128)(2,1)}, u32[]{:S(2)}) copy-start(bf16[2,2,24,1536]{3,2,1,0:T(8,128)(2,1)} %param.58) | copy-start | bytes 884740
  596.7 10.6 %collective-permute-start.3 = (bf16[1,2,24,1536]{3,2,1,0:T(8,128)(2,1)}, bf16[1,2,24,1536]{3,2,1,0:T(8,128)(2,1)S(1)}, u32[]{:S(2)}, u32[]{:S(2)}) collective-permute-start(bf16[1,2,24,1536]{3,2,1,0:T(8,128)(2,1)} %get-tuple-element.2102), channel_id=1, source_target_pairs={{0,64},{64,128},{128,192},{1,65},{65,129},{129,193},{2,66},{66,130... | collective-permute-start | bytes 442376 | tf_op jit(solution)/shard_map/ppermute | solution.py:12
  606.0 2.8 copy-start.12
  607.3 2.2 copy-start.10
  608.0 2.2 copy-start.8
  608.0 2.9 copy-start.6
  611.7 6.4 %copy-start.15 = (f32[1,1,24,1536]{3,2,1,0:T(8,128)S(1)}, f32[1,1,24,1536]{3,2,1,0:T(8,128)}, u32[]{:S(2)}) copy-start(f32[1,1,24,1536]{3,2,1,0:T(8,128)} %get-tuple-element.2054) | copy-start | bytes 442372
  611.7 6.4 %copy-start.16 = (f32[1,1,24,1536]{3,2,1,0:T(8,128)S(1)}, f32[1,1,24,1536]{3,2,1,0:T(8,128)}, u32[]{:S(2)}) copy-start(f32[1,1,24,1536]{3,2,1,0:T(8,128)} %get-tuple-element.2058) | copy-start | bytes 442372
  (11 other events, 7.8 us)
where the time goes:
time: 631 us; the launch traced here: 621 us
  starting transfers between devices  241 us (38%)
  local copies, waits for them, and re-layouts  192 us (30%)
  waiting for transfers between devices  110 us (17%)
  matrix products  39.3 us (6%)
  other arithmetic  30.7 us (5%)
    all_to_all x9, starting transfers between devices, propagate(): lax.all_to_all(spectrum_rows, 'slab', split_axis=3, concat_axis=2, tiled=...  90.4 us
    ppermute x8, starting transfers between devices, from_behind(): return lax.ppermute(block, axis, route)  77 us
    all_to_all x9, starting transfers between devices, propagate(): lax.all_to_all(filtered, 'slab', split_axis=2, concat_axis=3, tiled=True)  73.7 us
    unnamed x102, local copies, waits for them, and re-layouts  73.6 us
    ppermute x8, waiting for transfers between devices, from_behind(): return lax.ppermute(block, axis, route)  52.9 us
    another operation x49, local copies, waits for them, and re-layouts  45.1 us
    all_to_all x9, waiting for transfers between devices, propagate(): lax.all_to_all(filtered, 'slab', split_axis=2, concat_axis=3, tiled=True)  28.4 us
    all_to_all x9, waiting for transfers between devices, propagate(): lax.all_to_all(spectrum_rows, 'slab', split_axis=3, concat_axis=2, tiled=...  28.3 us
  transfers between devices with their start and end apart: 26, of which 12 were waited for; matrix products, arithmetic and copies ran while one was open for 29% of the time, Pallas kernels for 0%

commit v1 on v0

v1 whole, which is shorter than its diff:
```python
import functools
import math

import jax
import jax.numpy as jnp
import numpy as np
from jax import lax
from jax.experimental import pallas as pl
from jax.experimental.pallas import tpu as pltpu
from jax.sharding import PartitionSpec as P

N = 1536
SLABS = 64
ROWS = N // SLABS
BIG = 256
SMALL = N // BIG
KEEP = BIG // SLABS
DEPTH = 4
MESH = pl.DeviceIdType.MESH
F32 = jnp.float32
BF16 = jnp.bfloat16


def angle(x, period):
    turn = 2.0 * math.pi * (x % period) / period
    return np.cos(turn), np.sin(turn)


def block_matrix(re_re, re_im, im_re, im_im):
    return np.block([[re_re, re_im], [im_re, im_im]])


@functools.lru_cache(None)
def make_tables():
    bf = lambda a: np.asarray(a, np.float32).astype(jnp.bfloat16)
    freq = np.arange(BIG)
    samp = np.arange(BIG)
    cos, sin = angle(freq[:, None] * samp[None, :], BIG)
    full = np.zeros((SLABS, 2, KEEP, 2, BIG))
    c4, s4 = cos.reshape(SLABS, KEEP, BIG), sin.reshape(SLABS, KEEP, BIG)
    full[:, 0, :, 0], full[:, 0, :, 1] = c4, s4
    full[:, 1, :, 0], full[:, 1, :, 1] = -s4, c4
    row_fwd = full.reshape(512, 512)
    full = np.zeros((SLABS, 2, KEEP, 2, BIG))
    full[:, 0, :, 0], full[:, 0, :, 1] = c4, s4
    full[:, 1, :, 0], full[:, 1, :, 1] = -s4, c4
    row_inv = full.reshape(512, 512)
    m64 = np.arange(SLABS)
    cos, sin = angle(m64[:, None] * m64[None, :], SLABS)
    full = np.zeros((2, KEEP, SLABS, SLABS, 2, KEEP))
    back = np.zeros((SLABS, 2, KEEP, 2, KEEP, SLABS))
    for k in range(KEEP):
        full[0, k, :, :, 0, k], full[0, k, :, :, 1, k] = cos, sin
        full[1, k, :, :, 0, k], full[1, k, :, :, 1, k] = -sin, cos
        back[:, 0, k, 0, k, :], back[:, 0, k, 1, k, :] = cos, -sin
        back[:, 1, k, 0, k, :], back[:, 1, k, 1, k, :] = sin, cos
    col_fwd = full.reshape(512, 512)
    col_inv = back.reshape(512, 512)
    lane_fwd = np.zeros((2, 256, 2, 256))
    lane_inv = np.zeros((2, 256, 2, 256))
    rho = np.arange(ROWS)
    cos, sin = angle(rho[:, None] * rho[None, :], ROWS)
    for j in range(SMALL):
        a = 24 * j + rho[:, None]
        b = 8 * rho[None, :] + j
        lane_fwd[0, a, 0, b], lane_fwd[1, a, 0, b] = cos, sin
        lane_fwd[0, a, 1, b], lane_fwd[1, a, 1, b] = -sin, cos
        lane_inv[0, b, 0, a], lane_inv[1, b, 0, a] = cos, -sin
        lane_inv[0, b, 1, a], lane_inv[1, b, 1, a] = sin, cos
    lane_fwd = lane_fwd.reshape(512, 512)
    lane_inv = lane_inv.reshape(512, 512)
    cos, sin = angle(np.arange(SMALL)[:, None] * samp[None, :], N)
    row_tw = np.zeros((2, 8, BIG))
    row_tw[0, :SMALL], row_tw[1, :SMALL] = cos, sin
    cos, sin = angle(m64[:, None] * rho[None, :], N)
    col_tw = np.zeros((2, SLABS, 256))
    for j in range(SMALL):
        col_tw[0, :, 24 * j : 24 * j + 24] = cos
        col_tw[1, :, 24 * j : 24 * j + 24] = sin
    mats = np.stack([row_fwd, col_fwd, lane_fwd, lane_inv, col_inv, row_inv])
    return bf(mats), row_tw.astype(np.float32), col_tw.astype(np.float32)


def dot(a, b, dims=((1,), (0,))):
    return lax.dot_general(a, b, (dims, ((), ())), preferred_element_type=F32)


def dft_three(x, orient):
    (ar, ai), (br, bi), (cr, ci) = x
    tr, ti = br + cr, bi + ci
    er, ei = (br - cr) * (orient * math.sqrt(0.75)), (bi - ci) * (orient * math.sqrt(0.75))
    mr, mi = ar - 0.5 * tr, ai - 0.5 * ti
    return (ar + tr, ai + ti), (mr + ei, mi - er), (mr - ei, mi + er)


def dft_six(x, orient):
    out = [None] * 6
    for k1 in range(2):
        sums = []
        for n2 in range(3):
            (ar, ai), (br, bi) = x[(2 * n2) % 6], x[(3 + 2 * n2) % 6]
            sums.append((ar + br, ai + bi) if k1 == 0 else (ar - br, ai - bi))
        three = dft_three(sums, orient)
        for k2 in range(3):
            out[(3 * k1 + 4 * k2) % 6] = three[k2]
    return out


def pack(y):
    both = [y[:, :128].reshape(SLABS, 8, 128), y[:, 128:].reshape(SLABS, 8, 128)]
    return jnp.concatenate(both, axis=1).astype(BF16)


def unpack(x):
    x = x.astype(F32)
    both = [x[:, :8].reshape(512, 128), x[:, 8:].reshape(512, 128)]
    return jnp.concatenate(both, axis=1).astype(BF16)


def hop(a, n):
    return min(a, n - a)


def slab_order():
    offs = [(y, z, c) for y in range(4) for z in range(8) for c in range(2)][1:]
    offs.sort(key=lambda t: (-(hop(t[0], 4) + hop(t[1], 8)), t[2], t[1], t[0]))
    plus = [t for t in offs if 0 < t[1] < 4]
    minus = [t for t in offs if t[1] > 4]
    rest = [t for t in offs if t[1] in (0, 4)]
    out = []
    for i in range(len(plus)):
        out += [plus[i], minus[i]] + rest[i : i + 1]
    return out + rest[len(plus) :]


def kernel(inc, trans, phase, cot, mats, row_tw, col_tw, out,
           tbuf, cur, zbuf, send1, recv1, send2, recv2, results, hbuf, pbuf, outgoing,
           a2a_send, a2a_recv, t_send, t_recv, r_send, r_recv):
    depth = lax.axis_index("depth")
    slab = lax.axis_index("slab")
    y0, z0, c0 = slab // 16, (slab // 2) % 8, slab % 2
    forward = depth >= 2
    adjoint = depth < 2
    partners = [
        lax.rem(y0 + dy, 4) * 16 + lax.rem(z0 + dz, 8) * 2 + lax.rem(c0 + dc, 2)
        for dy, dz, dc in slab_order()
    ]
    others = [lax.rem(depth + o, DEPTH) for o in range(1, DEPTH)]

    barrier = pltpu.get_barrier_semaphore()
    for p in partners:
        pl.semaphore_signal(barrier, inc=1, device_id=(depth, p), device_id_type=MESH)
    for d in others:
        pl.semaphore_signal(barrier, inc=1, device_id=(d, slab), device_id_type=MESH)

    tbuf[depth] = trans[...]
    zbuf[144:, :] = jnp.zeros((112, 512), F32)

    @pl.when(adjoint)
    def _():
        cur[...] = cot[lax.rem(depth, 2)].astype(F32)

    @pl.when(depth == 0)
    def _():
        results[2] = inc[0]
        results[3] = inc[1]

    pl.semaphore_wait(barrier, len(partners) + len(others))

    def t_copy(d):
        return pltpu.make_async_remote_copy(
            src_ref=trans, dst_ref=tbuf.at[depth], send_sem=t_send.at[d], recv_sem=t_recv.at[depth],
            device_id=(d, slab), device_id_type=MESH)

    def t_needed(source, target):
        return jnp.where(target < 2, source >= 1, source <= 2)

    for d in others:
        @pl.when(t_needed(depth, d))
        def _(d=d):
            t_copy(d).start()

    def t_arrived(which):
        @pl.when(which != depth)
        def _():
            pltpu.make_async_copy(trans, tbuf.at[which], t_recv.at[which]).wait()

    orient = jnp.where(forward, 1.0, -1.0).astype(F32)

    def multiply(field, which):
        f = field.astype(F32)
        t = tbuf[which].astype(F32)
        fr, fi, tr, ti = f[:ROWS], f[ROWS:], t[:ROWS], t[ROWS:] * orient
        cur[:ROWS] = (fr * tr - fi * ti).astype(BF16).astype(F32)
        cur[ROWS:] = (fr * ti + fi * tr).astype(BF16).astype(F32)

    @pl.when(forward)
    def _():
        t_arrived(0)
        multiply(inc[lax.rem(depth, 2)], 0)

    def exchange(which, sent, received):
        for p in partners:
            pltpu.make_async_remote_copy(
                src_ref=sent.at[p], dst_ref=received.at[slab], send_sem=a2a_send.at[which],
                recv_sem=a2a_recv.at[which], device_id=(depth, p), device_id_type=MESH).start()
        received[slab] = sent[slab]

    def finish(which, sent, received):
        part = received.at[pl.ds(0, SLABS - 1)]
        pltpu.make_async_copy(part, part, a2a_recv.at[which]).wait()
        part = sent.at[pl.ds(0, SLABS - 1)]
        pltpu.make_async_copy(part, part, a2a_send.at[which]).wait()

    def stage_a():
        for half in range(2):
            lo = 128 * half
            x = [(cur[:ROWS, BIG * a + lo : BIG * a + lo + 128], cur[ROWS:, BIG * a + lo : BIG * a + lo + 128])
                 for a in range(SMALL)]
            for j, (zr, zi) in enumerate(dft_six(x, 1.0)):
                c = row_tw[0, j : j + 1, lo : lo + 128]
                s = row_tw[1, j : j + 1, lo : lo + 128]
                zbuf[ROWS * j : ROWS * j + ROWS, lo : lo + 128] = zr * c + zi * s
                zbuf[ROWS * j : ROWS * j + ROWS, BIG + lo : BIG + lo + 128] = zi * c - zr * s
        send1[...] = pack(dot(mats[0], zbuf[...].astype(BF16), ((1,), (1,))))

    def make_filter():
        lane = lax.broadcasted_iota(jnp.int32, (SLABS, 128), 1)
        for k in range(KEEP):
            for chunk in range(2):
                hbuf[0, 64 * k : 64 * k + 64, 128 * chunk : 128 * chunk + 128] = jnp.zeros((64, 128), F32)
        pbuf[...] = jnp.zeros_like(pbuf)
        for chunk, count in ((0, 16), (1, 8)):
            acc = [jnp.zeros((SLABS, 128), F32) for _ in range(KEEP)]
            for i in range(count):
                p = 16 * chunk + i
                pbuf[:, :ROWS] = phase[64 * p : 64 * p + 64, :]
                block = pbuf[...]
                inside = (lane >= 8 * i) & (lane < 8 * i + SMALL)
                for k in range(KEEP):
                    moved = pltpu.roll(block, (8 * i - SMALL * k) % 128, 1)
                    acc[k] = jnp.where(inside, moved, acc[k])
            for k in range(KEEP):
                hbuf[0, 64 * k : 64 * k + 64, 128 * chunk : 128 * chunk + 128] = jnp.cos(acc[k])
                hbuf[1, 64 * k : 64 * k + 64, 128 * chunk : 128 * chunk + 128] = jnp.sin(acc[k]) * orient

    def stage_b():
        y = dot(mats[1], unpack(recv1[...]))
        c, s = col_tw[0][None], col_tw[1][None]
        yr, yi = y[:256].reshape(KEEP, 64, 256), y[256:].reshape(KEEP, 64, 256)
        z = jnp.concatenate([(yr * c + yi * s).reshape(256, 256), (yi * c - yr * s).reshape(256, 256)], axis=1)
        y = dot(z.astype(BF16), mats[2])
        yr, yi, hr, hi = y[:, :256], y[:, 256:], hbuf[0], hbuf[1]
        z = jnp.concatenate([yr * hr - yi * hi, yi * hr + yr * hi], axis=1)
        y = dot(z.astype(BF16), mats[3])
        yr, yi = y[:, :256].reshape(KEEP, 64, 256), y[:, 256:].reshape(KEEP, 64, 256)
        c, s = c * (1.0 / N), s * (1.0 / N)
        z = jnp.concatenate([(yr * c - yi * s).reshape(256, 256), (yi * c + yr * s).reshape(256, 256)], axis=0)
        send2[...] = pack(dot(mats[4], z.astype(BF16)))

    def stage_c(turn):
        zbuf_c = dot(unpack(recv2[...]), mats[5], ((0,), (0,)))
        for half in range(2):
            lo = 128 * half
            x = []
            for j in range(SMALL):
                c = row_tw[0, j : j + 1, lo : lo + 128] * (1.0 / N)
                s = row_tw[1, j : j + 1, lo : lo + 128] * (1.0 / N)
                zr = zbuf_c[ROWS * j : ROWS * j + ROWS, lo : lo + 128]
                zi = zbuf_c[ROWS * j : ROWS * j + ROWS, BIG + lo : BIG + lo + 128]
                x.append((zr * c - zi * s, zi * c + zr * s))
            for a, (vr, vi) in enumerate(dft_six(x, -1.0)):
                both = jnp.concatenate([vr, vi], axis=0)
                outgoing[turn, :, BIG * a + lo : BIG * a + lo + 128] = both.astype(BF16)

    def r_copy(turn, target):
        return pltpu.make_async_remote_copy(
            src_ref=outgoing.at[turn], dst_ref=results.at[depth], send_sem=r_send.at[turn],
            recv_sem=r_recv.at[depth], device_id=(target, slab), device_id_type=MESH)

    def target_of(turn):
        return jnp.where(forward, turn + 1, DEPTH - 1 - turn)

    @pl.loop(0, DEPTH)
    def _(turn):
        @pl.when(adjoint | (turn < DEPTH - 1))
        def _():
            stage_a()
            exchange(0, send1, recv1)

            @pl.when(turn == 0)
            def _():
                make_filter()

            finish(0, send1, recv1)
            stage_b()
            exchange(1, send2, recv2)
            finish(1, send2, recv2)
            stage_c(turn)
            target = target_of(turn)

            @pl.when(target != depth)
            def _():
                r_copy(turn, target).start()

            @pl.when(target == depth)
            def _():
                results[depth] = outgoing[turn]

            @pl.when(jnp.where(forward, turn < DEPTH - 2, turn < DEPTH - 1))
            def _():
                t_arrived(target)
                multiply(outgoing[turn], target)

    for slot in range(DEPTH):
        @pl.when((depth != slot) & ((slot < 2) | (depth >= 1)))
        def _(slot=slot):
            pltpu.make_async_copy(trans, results.at[slot], r_recv.at[slot]).wait()

    gr = jnp.zeros((ROWS, N), F32)
    gi = jnp.zeros((ROWS, N), F32)
    for m in range(2):
        u = results[2 + m].astype(F32)
        p = results[m].astype(F32)
        ur, ui, pr, pi = u[:ROWS], u[ROWS:], p[:ROWS], p[ROWS:]
        gr = gr + (ur * pr + ui * pi)
        gi = gi + (ur * pi - ui * pr)
    out[:ROWS] = gr
    out[ROWS:] = gi

    for d in others:
        @pl.when(t_needed(depth, d))
        def _(d=d):
            t_copy(d).wait_send()

    for turn in range(DEPTH):
        target = target_of(turn)

        @pl.when((target != depth) & (adjoint | (turn < DEPTH - 1)))
        def _(turn=turn, target=target):
            r_copy(turn, target).wait_send()


def on_device(incident, transmission, prop_phase, cotangent):
    mats, row_tw, col_tw = (jnp.asarray(t) for t in make_tables())
    inc = incident.reshape(2, 2 * ROWS, N)
    trans = transmission.reshape(2 * ROWS, N)
    cot = cotangent.reshape(2, 2 * ROWS, N)
    vmem = pl.BlockSpec(memory_space=pltpu.VMEM)
    field = (2 * ROWS, N)
    message = (SLABS, 16, 128)
    dma = pltpu.SemaphoreType.DMA
    grads = pl.pallas_call(
        kernel,
        out_shape=jax.ShapeDtypeStruct(field, F32),
        in_specs=[vmem] * 7,
        out_specs=vmem,
        scratch_shapes=[
            pltpu.VMEM((DEPTH,) + field, BF16),
            pltpu.VMEM(field, F32),
            pltpu.VMEM((256, 512), F32),
            pltpu.VMEM(message, BF16),
            pltpu.VMEM(message, BF16),
            pltpu.VMEM(message, BF16),
            pltpu.VMEM(message, BF16),
            pltpu.VMEM((DEPTH,) + field, BF16),
            pltpu.VMEM((2, 256, 256), F32),
            pltpu.VMEM((SLABS, 128), F32),
            pltpu.VMEM((DEPTH,) + field, BF16),
            dma((2,)), dma((2,)), dma((DEPTH,)), dma((DEPTH,)), dma((DEPTH,)), dma((DEPTH,)),
        ],
        compiler_params=pltpu.CompilerParams(
            collective_id=0, has_side_effects=True, vmem_limit_bytes=48 * 2**20),
        name="chains",
    )(inc, trans, prop_phase, cot, mats, row_tw, col_tw)
    return grads.reshape(1, 2, ROWS, N)


def solution(mesh):
    in_specs = (
        P(None, None, "slab", None),
        P("depth", None, "slab", None),
        P(None, "slab"),
        P(None, None, "slab", None),
    )
    out_specs = P("depth", None, "slab", None)
    return jax.shard_map(
        on_device, mesh=mesh, in_specs=in_specs, out_specs=out_specs, check_vma=False
    )
```

time: 631 us -> 104 us (0.16); the launches traced: 621 us -> 104 us
  starting transfers between devices: 241 us -> 0 us
  local copies, waits for them, and re-layouts: 192 us -> 8.23 us
  waiting for transfers between devices: 110 us -> 0 us
  Pallas kernels: 0 us -> 96 us
  matrix products: 39.3 us -> 0 us
  other arithmetic: 30.7 us -> 0 us
    all_to_all x18 -> x0, starting transfers between devices: 164 us -> none  [the longest x9 90.4 us: propagate(): lax.all_to_all(spectrum_rows, 'slab', split_axis=3, concat_axis=2, tiled=...]
    pallas_call x0 -> x1, Pallas kernels: none -> 96 us  [on_device(): pl.pallas_call(kernel, out_shape=jax.ShapeDtypeStruct(field, F32), in_spe...]
    ppermute x8 -> x0, starting transfers between devices: 77 us -> none  [from_behind(): return lax.ppermute(block, axis, route)]
    unnamed x102 -> x14, local copies, waits for them, and re-layouts: 73.6 us -> 8.23 us
    another operation x89 -> x0, local copies, waits for them, and re-layouts: 60.1 us -> none
    all_to_all x18 -> x0, waiting for transfers between devices: 56.7 us -> none  [the longest x9 28.4 us: propagate(): lax.all_to_all(filtered, 'slab', split_axis=2, concat_axis=3, tiled=True)]
    ppermute x8 -> x0, waiting for transfers between devices: 52.9 us -> none  [from_behind(): return lax.ppermute(block, axis, route)]
    dot_general x56 -> x0, matrix products: 37.4 us -> none  [the longest x8 7.47 us: along_columns(): jnp.einsum('mzrka,aj->mzrjk', segment, small_cos, precision=lax.Precision...]
  transfers between devices with their start and end apart: 26 -> 0, of which waited for: 12 -> 0; matrix products, arithmetic and copies ran while one was open for 29% -> 0% of each run, Pallas kernels for 0% -> 0%
where the time goes in v1:
time: 104 us
  Pallas kernels  96 us (92%)
  local copies, waits for them, and re-layouts  8.23 us (8%)
    pallas_call x1, Pallas kernels, on_device(): pl.pallas_call(kernel, out_shape=jax.ShapeDtypeStruct(field, F32), in_spe...  96 us
    unnamed x14, local copies, waits for them, and re-layouts  8.23 us

profile of v1, /device:TPU:1, one launch (start us, length us, event | category | flops | bytes accessed | tf_op | source)
XLA Modules:
  0.0 104.2 jit_solution(10376202176031097755)
XLA Ops:
  0.0 1.2 %copy.8.phase = f32[1536,24]{1,0:T(8,128)S(1)} copy(f32[1536,24]{0,1:T(8,128)} %param.9) | data formatting | bytes 294912 | tf_op args[2]
  1.2 0.0 copy-start
  1.2 1.9 %copy-done = bf16[6,512,512]{2,1,0:T(8,128)(2,1)S(1)} copy-done((bf16[6,512,512]{2,1,0:T(8,128)(2,1)S(1)}, bf16[6,512,512]{2,1,0:T(8,128)(2,1)}, u32[]{:S(2)}) %copy-start) | copy-done | bytes 3145752
  3.1 0.0 copy-start.1
  3.1 1.0 copy-done.1
  4.0 0.0 copy-start.2
  4.0 1.0 copy-done.2
  5.0 0.0 copy-start.3
  5.0 0.9 copy-done.3
  5.9 0.0 copy-start.4
  5.9 0.9 copy-done.4
  6.8 0.0 copy-start.5
  6.8 0.7 copy-done.5
  7.5 96.0 %chains.1 = f32[48,1536]{1,0:T(8,128)S(1)} custom-call(bf16[2,48,1536]{2,1,0:T(8,128)(2,1)S(1)} %bitcast.5, bf16[48,1536]{1,0:T(8,128)(2,1)S(1)} %bitcast.7, f32[1536,24]{1,0:T(8,128)S(1)} %copy.8.phase, bf16[2,48,1536]{2,1,0:T(8,128)(2,1)S(1)} %bitcast.6, bf16[6,512,512]{2,1,0:T(8,128)(2,1)S(1)} %copy-done, f32[2,8,256]{2,1,0:T(8,128)S(1)} %copy-done.5, ...), custom_call_target="tpu_custom_call" | custom-call | tf_op jit(solution)/shard_map/chains/pallas_call | solution.py:353
  103.5 0.7 copy.10
Async XLA Ops:
  1.2 1.9 %copy-start = (bf16[6,512,512]{2,1,0:T(8,128)(2,1)S(1)}, bf16[6,512,512]{2,1,0:T(8,128)(2,1)}, u32[]{:S(2)}) copy-start(bf16[6,512,512]{2,1,0:T(8,128)(2,1)} %constant.6.clone.mats) | copy-start | bytes 9437188
  3.1 1.0 copy-start.1
  4.0 1.0 copy-start.2
  5.0 0.9 copy-start.3
  5.9 0.9 copy-start.4
  6.8 0.7 copy-start.5

commit v2 on v1

--- a/solution.py
+++ b/solution.py
@@ -106,14 +106,21 @@
     return out
 
 
-def pack(y):
-    both = [y[:, :128].reshape(SLABS, 8, 128), y[:, 128:].reshape(SLABS, 8, 128)]
-    return jnp.concatenate(both, axis=1).astype(BF16)
-
-
-def unpack(x):
-    x = x.astype(F32)
-    both = [x[:, :8].reshape(512, 128), x[:, 8:].reshape(512, 128)]
+def pack(y, main, rest, fold):
+    main[...] = y[:, :128].reshape(SLABS, 8, 128).astype(BF16)
+    fold[...] = y[:, 128:]
+    row = fold[pl.ds(0, SLABS, stride=8), :]
+    for i in range(1, 8):
+        row = row + pltpu.roll(fold[pl.ds(i, SLABS, stride=8), :], 16 * i, 1)
+    rest[...] = row.reshape(SLABS, 1, 128)
+
+
+def unpack(main, rest, fold):
+    row = rest[...].reshape(SLABS, 128)
+    fold[pl.ds(0, SLABS, stride=8), :] = row
+    for i in range(1, 8):
+        fold[pl.ds(i, SLABS, stride=8), :] = pltpu.roll(row, 128 - 16 * i, 1)
+    both = [main[...].astype(F32).reshape(512, 128), fold[...]]
     return jnp.concatenate(both, axis=1).astype(BF16)
 
 
@@ -133,84 +140,93 @@
     return out + rest[len(plus) :]
 
 
-def kernel(inc, trans, phase, cot, mats, row_tw, col_tw, out,
-           tbuf, cur, zbuf, send1, recv1, send2, recv2, results, hbuf, pbuf, outgoing,
-           a2a_send, a2a_recv, t_send, t_recv, r_send, r_recv):
+def kernel(inc_hbm, trans_hbm, phase_hbm, cot_hbm, mats_hbm, row_tw_hbm, col_tw_hbm, out,
+           field, phase, mats, row_tw, col_tw,
+           tbuf, cur, zbuf, fold, send1, send1r, recv1, recv1r, send2, send2r, recv2, recv2r,
+           results, hbuf, pbuf, outgoing,
+           load, load_mat, a2a_send, a2a_recv, t_send, t_recv, r_send, r_recv):
     depth = lax.axis_index("depth")
     slab = lax.axis_index("slab")
     y0, z0, c0 = slab // 16, (slab // 2) % 8, slab % 2
     forward = depth >= 2
     adjoint = depth < 2
+    which_field = lax.rem(depth, 2)
     partners = [
         lax.rem(y0 + dy, 4) * 16 + lax.rem(z0 + dz, 8) * 2 + lax.rem(c0 + dc, 2)
         for dy, dz, dc in slab_order()
     ]
     others = [lax.rem(depth + o, DEPTH) for o in range(1, DEPTH)]
 
+    @pl.when(adjoint)
+    def _():
+        pltpu.make_async_copy(cot_hbm.at[which_field], field, load.at[0]).start()
+
+    @pl.when(forward)
+    def _():
+        pltpu.make_async_copy(inc_hbm.at[which_field], field, load.at[0]).start()
+
+    loads = [
+        pltpu.make_async_copy(row_tw_hbm, row_tw, load.at[1]),
+        pltpu.make_async_copy(col_tw_hbm, col_tw, load.at[2]),
+        pltpu.make_async_copy(phase_hbm, phase, load.at[3]),
+        pltpu.make_async_copy(trans_hbm, tbuf.at[depth], load.at[4]),
+    ]
+    mat_loads = [pltpu.make_async_copy(mats_hbm.at[k], mats.at[k], load_mat.at[k]) for k in range(6)]
+    loads[0].start()
+    mat_loads[0].start()
+    for copy in loads[1:] + mat_loads[1:]:
+        copy.start()
+
+    @pl.when(depth == 0)
+    def _():
+        for m in range(2):
+            pltpu.make_async_copy(inc_hbm.at[m], results.at[2 + m], load.at[5 + m]).start()
+
     barrier = pltpu.get_barrier_semaphore()
     for p in partners:
         pl.semaphore_signal(barrier, inc=1, device_id=(depth, p), device_id_type=MESH)
     for d in others:
         pl.semaphore_signal(barrier, inc=1, device_id=(d, slab), device_id_type=MESH)
 
-    tbuf[depth] = trans[...]
     zbuf[144:, :] = jnp.zeros((112, 512), F32)
-
-    @pl.when(adjoint)
-    def _():
-        cur[...] = cot[lax.rem(depth, 2)].astype(F32)
-
-    @pl.when(depth == 0)
-    def _():
-        results[2] = inc[0]
-        results[3] = inc[1]
-
-    pl.semaphore_wait(barrier, len(partners) + len(others))
+    orient = jnp.where(forward, 1.0, -1.0).astype(F32)
 
     def t_copy(d):
         return pltpu.make_async_remote_copy(
-            src_ref=trans, dst_ref=tbuf.at[depth], send_sem=t_send.at[d], recv_sem=t_recv.at[depth],
+            src_ref=trans_hbm, dst_ref=tbuf.at[depth], send_sem=t_send.at[d], recv_sem=t_recv.at[depth],
             device_id=(d, slab), device_id_type=MESH)
 
     def t_needed(source, target):
         return jnp.where(target < 2, source >= 1, source <= 2)
-
-    for d in others:
-        @pl.when(t_needed(depth, d))
-        def _(d=d):
-            t_copy(d).start()
 
     def t_arrived(which):
         @pl.when(which != depth)
         def _():
-            pltpu.make_async_copy(trans, tbuf.at[which], t_recv.at[which]).wait()
-
-    orient = jnp.where(forward, 1.0, -1.0).astype(F32)
-
-    def multiply(field, which):
-        f = field.astype(F32)
+            pltpu.make_async_copy(field, tbuf.at[which], t_recv.at[which]).wait()
+
+    def multiply(values, which):
+        f = values.astype(F32)
         t = tbuf[which].astype(F32)
         fr, fi, tr, ti = f[:ROWS], f[ROWS:], t[:ROWS], t[ROWS:] * orient
         cur[:ROWS] = (fr * tr - fi * ti).astype(BF16).astype(F32)
         cur[ROWS:] = (fr * ti + fi * tr).astype(BF16).astype(F32)
 
-    @pl.when(forward)
-    def _():
-        t_arrived(0)
-        multiply(inc[lax.rem(depth, 2)], 0)
-
-    def exchange(which, sent, received):
+    def exchange(which, sent, sent_rest, received, received_rest):
         for p in partners:
             pltpu.make_async_remote_copy(
-                src_ref=sent.at[p], dst_ref=received.at[slab], send_sem=a2a_send.at[which],
-                recv_sem=a2a_recv.at[which], device_id=(depth, p), device_id_type=MESH).start()
+                src_ref=sent.at[p], dst_ref=received.at[slab], send_sem=a2a_send.at[which, 0],
+                recv_sem=a2a_recv.at[which, 0], device_id=(depth, p), device_id_type=MESH).start()
+            pltpu.make_async_remote_copy(
+                src_ref=sent_rest.at[p], dst_ref=received_rest.at[slab], send_sem=a2a_send.at[which, 1],
+                recv_sem=a2a_recv.at[which, 1], device_id=(depth, p), device_id_type=MESH).start()
         received[slab] = sent[slab]
-
-    def finish(which, sent, received):
-        part = received.at[pl.ds(0, SLABS - 1)]
-        pltpu.make_async_copy(part, part, a2a_recv.at[which]).wait()
-        part = sent.at[pl.ds(0, SLABS - 1)]
-        pltpu.make_async_copy(part, part, a2a_send.at[which]).wait()
+        received_rest[slab] = sent_rest[slab]
+
+    def finish(which, sent, sent_rest, received, received_rest):
+        for k, ref, sem in ((0, sent, a2a_send), (1, sent_rest, a2a_send),
+                            (0, received, a2a_recv), (1, received_rest, a2a_recv)):
+            part = ref.at[pl.ds(0, SLABS - 1)]
+            pltpu.make_async_copy(part, part, sem.at[which, k]).wait()
 
     def stage_a():
         for half in range(2):
@@ -222,20 +238,19 @@
                 s = row_tw[1, j : j + 1, lo : lo + 128]
                 zbuf[ROWS * j : ROWS * j + ROWS, lo : lo + 128] = zr * c + zi * s
                 zbuf[ROWS * j : ROWS * j + ROWS, BIG + lo : BIG + lo + 128] = zi * c - zr * s
-        send1[...] = pack(dot(mats[0], zbuf[...].astype(BF16), ((1,), (1,))))
+        pack(dot(mats[0], zbuf[...].astype(BF16), ((1,), (1,))), send1, send1r, fold)
 
     def make_filter():
         lane = lax.broadcasted_iota(jnp.int32, (SLABS, 128), 1)
-        for k in range(KEEP):
-            for chunk in range(2):
-                hbuf[0, 64 * k : 64 * k + 64, 128 * chunk : 128 * chunk + 128] = jnp.zeros((64, 128), F32)
         pbuf[...] = jnp.zeros_like(pbuf)
         for chunk, count in ((0, 16), (1, 8)):
             acc = [jnp.zeros((SLABS, 128), F32) for _ in range(KEEP)]
             for i in range(count):
-                p = 16 * chunk + i
-                pbuf[:, :ROWS] = phase[64 * p : 64 * p + 64, :]
-                block = pbuf[...]
+                if i % 2 == 0:
+                    lo = 64 * (16 * chunk + i)
+                    pbuf[:ROWS] = phase[:, lo : lo + 128]
+                    turned = pbuf[...].T
+                block = turned[64 * (i % 2) : 64 * (i % 2) + 64]
                 inside = (lane >= 8 * i) & (lane < 8 * i + SMALL)
                 for k in range(KEEP):
                     moved = pltpu.roll(block, (8 * i - SMALL * k) % 128, 1)
@@ -245,7 +260,7 @@
                 hbuf[1, 64 * k : 64 * k + 64, 128 * chunk : 128 * chunk + 128] = jnp.sin(acc[k]) * orient
 
     def stage_b():
-        y = dot(mats[1], unpack(recv1[...]))
+        y = dot(mats[1], unpack(recv1, recv1r, fold))
         c, s = col_tw[0][None], col_tw[1][None]
         yr, yi = y[:256].reshape(KEEP, 64, 256), y[256:].reshape(KEEP, 64, 256)
         z = jnp.concatenate([(yr * c + yi * s).reshape(256, 256), (yi * c - yr * s).reshape(256, 256)], axis=1)
@@ -256,10 +271,10 @@
         yr, yi = y[:, :256].reshape(KEEP, 64, 256), y[:, 256:].reshape(KEEP, 64, 256)
         c, s = c * (1.0 / N), s * (1.0 / N)
         z = jnp.concatenate([(yr * c - yi * s).reshape(256, 256), (yi * c + yr * s).reshape(256, 256)], axis=0)
-        send2[...] = pack(dot(mats[4], z.astype(BF16)))
+        pack(dot(mats[4], z.astype(BF16)), send2, send2r, fold)
 
     def stage_c(turn):
-        zbuf_c = dot(unpack(recv2[...]), mats[5], ((0,), (0,)))
+        zbuf_c = dot(unpack(recv2, recv2r, fold), mats[5], ((0,), (0,)))
         for half in range(2):
             lo = 128 * half
             x = []
@@ -281,21 +296,45 @@
     def target_of(turn):
         return jnp.where(forward, turn + 1, DEPTH - 1 - turn)
 
+    pltpu.make_async_copy(inc_hbm.at[0], field, load.at[0]).wait()
+    loads[0].wait()
+    mat_loads[0].wait()
+
+    @pl.when(adjoint)
+    def _():
+        cur[...] = field[...].astype(F32)
+        stage_a()
+
+    loads[3].wait()
+    loads[2].wait()
+    make_filter()
+    pl.semaphore_wait(barrier, len(partners) + len(others))
+
+    for d in others:
+        @pl.when(t_needed(depth, d))
+        def _(d=d):
+            t_copy(d).start()
+
+    @pl.when(forward)
+    def _():
+        t_arrived(0)
+        multiply(field[...], 0)
+        stage_a()
+
+    for copy in loads[1:2] + mat_loads[1:]:
+        copy.wait()
+
     @pl.loop(0, DEPTH)
     def _(turn):
         @pl.when(adjoint | (turn < DEPTH - 1))
         def _():
-            stage_a()
-            exchange(0, send1, recv1)
-
-            @pl.when(turn == 0)
-            def _():
-                make_filter()
-
-            finish(0, send1, recv1)
+            first = send1, send1r, recv1, recv1r
+            second = send2, send2r, recv2, recv2r
+            exchange(0, *first)
+            finish(0, *first)
             stage_b()
-            exchange(1, send2, recv2)
-            finish(1, send2, recv2)
+            exchange(1, *second)
+            finish(1, *second)
             stage_c(turn)
             target = target_of(turn)
 
@@ -311,11 +350,17 @@
             def _():
                 t_arrived(target)
                 multiply(outgoing[turn], target)
+                stage_a()
+
+    @pl.when(depth == 0)
+    def _():
+        for m in range(2):
+            pltpu.make_async_copy(inc_hbm.at[m], results.at[2 + m], load.at[5 + m]).wait()
 
     for slot in range(DEPTH):
         @pl.when((depth != slot) & ((slot < 2) | (depth >= 1)))
         def _(slot=slot):
-            pltpu.make_async_copy(trans, results.at[slot], r_recv.at[slot]).wait()
+            pltpu.make_async_copy(field, results.at[slot], r_recv.at[slot]).wait()
 
     gr = jnp.zeros((ROWS, N), F32)
     gi = jnp.zeros((ROWS, N), F32)
@@ -346,33 +391,38 @@
     inc = incident.reshape(2, 2 * ROWS, N)
     trans = transmission.reshape(2 * ROWS, N)
     cot = cotangent.reshape(2, 2 * ROWS, N)
-    vmem = pl.BlockSpec(memory_space=pltpu.VMEM)
+    hbm = pl.BlockSpec(memory_space=pltpu.HBM)
     field = (2 * ROWS, N)
-    message = (SLABS, 16, 128)
+    main = pltpu.VMEM((SLABS, 8, 128), BF16)
+    rest = pltpu.VMEM((SLABS, 1, 128), F32)
     dma = pltpu.SemaphoreType.DMA
     grads = pl.pallas_call(
         kernel,
         out_shape=jax.ShapeDtypeStruct(field, F32),
-        in_specs=[vmem] * 7,
-        out_specs=vmem,
+        in_specs=[hbm] * 7,
+        out_specs=pl.BlockSpec(memory_space=pltpu.VMEM),
         scratch_shapes=[
+            pltpu.VMEM(field, BF16),
+            pltpu.VMEM((ROWS, N), F32),
+            pltpu.VMEM(mats.shape, BF16),
+            pltpu.VMEM(row_tw.shape, F32),
+            pltpu.VMEM(col_tw.shape, F32),
             pltpu.VMEM((DEPTH,) + field, BF16),
             pltpu.VMEM(field, F32),
             pltpu.VMEM((256, 512), F32),
-            pltpu.VMEM(message, BF16),
-            pltpu.VMEM(message, BF16),
-            pltpu.VMEM(message, BF16),
-            pltpu.VMEM(message, BF16),
+            pltpu.VMEM((512, 128), F32),
+            main, rest, main, rest, main, rest, main, rest,
             pltpu.VMEM((DEPTH,) + field, BF16),
             pltpu.VMEM((2, 256, 256), F32),
-            pltpu.VMEM((SLABS, 128), F32),
+            pltpu.VMEM((128, 128), F32),
             pltpu.VMEM((DEPTH,) + field, BF16),
-            dma((2,)), dma((2,)), dma((DEPTH,)), dma((DEPTH,)), dma((DEPTH,)), dma((DEPTH,)),
+            dma((7,)), dma((6,)), dma((2, 2)), dma((2, 2)),
+            dma((DEPTH,)), dma((DEPTH,)), dma((DEPTH,)), dma((DEPTH,)),
         ],
         compiler_params=pltpu.CompilerParams(
-            collective_id=0, has_side_effects=True, vmem_limit_bytes=48 * 2**20),
+            collective_id=0, has_side_effects=True, vmem_limit_bytes=62 * 2**20),
         name="chains",
-    )(inc, trans, prop_phase, cot, mats, row_tw, col_tw)
+    )(inc, trans, prop_phase.T, cot, mats, row_tw, col_tw)
     return grads.reshape(1, 2, ROWS, N)
 
 

time: 104 us -> 85.3 us (0.82)
  Pallas kernels: 96 us -> 83.5 us
  local copies, waits for them, and re-layouts: 8.23 us -> 1.69 us
    pallas_call x1, Pallas kernels: 96 us -> 83.5 us  [on_device(): pl.pallas_call(kernel, out_shape=jax.ShapeDtypeStruct(field, F32), in_spe...]
    unnamed x14 -> x1, local copies, waits for them, and re-layouts: 8.23 us -> 1.69 us
where the time goes in v2:
time: 85.3 us; the launch traced here: 85.2 us
  Pallas kernels  83.5 us (98%)
  local copies, waits for them, and re-layouts  1.69 us (2%)
    pallas_call x1, Pallas kernels, on_device(): pl.pallas_call(kernel, out_shape=jax.ShapeDtypeStruct(field, F32), in_spe...  83.5 us

profile of v2, /device:TPU:1, one launch (start us, length us, event | category | flops | bytes accessed | tf_op | source)
XLA Modules:
  0.0 85.2 jit_solution(14942368127833391254)
XLA Ops:
  0.0 83.5 %chains.1 = f32[48,1536]{1,0:T(8,128)} custom-call(bf16[2,48,1536]{2,1,0:T(8,128)(2,1)} %bitcast.6, bf16[48,1536]{1,0:T(8,128)(2,1)} %bitcast.8, f32[24,1536]{1,0:T(8,128)} %bitcast.9, bf16[2,48,1536]{2,1,0:T(8,128)(2,1)} %bitcast.7, bf16[6,512,512]{2,1,0:T(8,128)(2,1)} %constant.6.clone.mats_hbm, f32[2,8,256]{2,1,0:T(8,128)} %constant.7.clone.row_tw_hbm, ...), custom_call_target="tpu_custom_call" | custom-call | tf_op jit(solution)/shard_map/chains/pallas_call | solution.py:399
  83.5 1.7 %copy.9 = f32[1,2,24,1536]{3,2,1,0:T(8,128)} copy(f32[1,2,24,1536]{3,2,1,0:T(8,128)} %bitcast.5) | data formatting | bytes 589824

commit v3 on v2

--- a/solution.py
+++ b/solution.py
@@ -56,29 +56,27 @@
         back[:, 1, k, 0, k, :], back[:, 1, k, 1, k, :] = sin, cos
     col_fwd = full.reshape(512, 512)
     col_inv = back.reshape(512, 512)
-    lane_fwd = np.zeros((2, 256, 2, 256))
-    lane_inv = np.zeros((2, 256, 2, 256))
+    half_fwd = np.zeros((2, 192, 2, 144))
+    half_inv = np.zeros((2, 144, 2, 192))
     rho = np.arange(ROWS)
     cos, sin = angle(rho[:, None] * rho[None, :], ROWS)
     for j in range(SMALL):
-        a = 24 * j + rho[:, None]
-        b = 8 * rho[None, :] + j
-        lane_fwd[0, a, 0, b], lane_fwd[1, a, 0, b] = cos, sin
-        lane_fwd[0, a, 1, b], lane_fwd[1, a, 1, b] = -sin, cos
-        lane_inv[0, b, 0, a], lane_inv[1, b, 0, a] = cos, -sin
-        lane_inv[0, b, 1, a], lane_inv[1, b, 1, a] = sin, cos
-    lane_fwd = lane_fwd.reshape(512, 512)
-    lane_inv = lane_inv.reshape(512, 512)
+        a = 24 * j + rho[None, :]
+        b = 8 * rho[:, None] + j
+        half_fwd[0, b, 0, a], half_fwd[0, b, 1, a] = cos, sin
+        half_fwd[1, b, 0, a], half_fwd[1, b, 1, a] = -sin, cos
+        half_inv[0, a, 0, b], half_inv[0, a, 1, b] = cos, -sin
+        half_inv[1, a, 0, b], half_inv[1, a, 1, b] = sin, cos
+    half_fwd = half_fwd.reshape(384, 288)
+    half_inv = half_inv.reshape(288, 384)
     cos, sin = angle(np.arange(SMALL)[:, None] * samp[None, :], N)
     row_tw = np.zeros((2, 8, BIG))
     row_tw[0, :SMALL], row_tw[1, :SMALL] = cos, sin
-    cos, sin = angle(m64[:, None] * rho[None, :], N)
-    col_tw = np.zeros((2, SLABS, 256))
-    for j in range(SMALL):
-        col_tw[0, :, 24 * j : 24 * j + 24] = cos
-        col_tw[1, :, 24 * j : 24 * j + 24] = sin
-    mats = np.stack([row_fwd, col_fwd, lane_fwd, lane_inv, col_inv, row_inv])
-    return bf(mats), row_tw.astype(np.float32), col_tw.astype(np.float32)
+    cos, sin = angle(rho[:, None] * m64[None, :], N)
+    col_tw = np.stack([np.tile(cos, (1, KEEP)), np.tile(sin, (1, KEEP))])
+    mats = np.stack([row_fwd, col_fwd.T, col_inv, row_inv])
+    f32 = lambda a: np.asarray(a, np.float32)
+    return bf(mats), bf(half_fwd), bf(half_inv), f32(row_tw), f32(col_tw)
 
 
 def dot(a, b, dims=((1,), (0,))):
@@ -140,10 +138,10 @@
     return out + rest[len(plus) :]
 
 
-def kernel(inc_hbm, trans_hbm, phase_hbm, cot_hbm, mats_hbm, row_tw_hbm, col_tw_hbm, out,
-           field, phase, mats, row_tw, col_tw,
+def kernel(inc_hbm, trans_hbm, phase_hbm, cot_hbm, mats_hbm, half_fwd_hbm, half_inv_hbm, row_tw_hbm,
+           col_tw_hbm, out, field, phase, mats, half_fwd, half_inv, row_tw, col_tw,
            tbuf, cur, zbuf, fold, send1, send1r, recv1, recv1r, send2, send2r, recv2, recv2r,
-           results, hbuf, pbuf, outgoing,
+           recv3, recv3r, results, hbuf, outgoing,
            load, load_mat, a2a_send, a2a_recv, t_send, t_recv, r_send, r_recv):
     depth = lax.axis_index("depth")
     slab = lax.axis_index("slab")
@@ -157,6 +155,12 @@
     ]
     others = [lax.rem(depth + o, DEPTH) for o in range(1, DEPTH)]
 
+    barrier = pltpu.get_barrier_semaphore()
+    for p in partners:
+        pl.semaphore_signal(barrier, inc=1, device_id=(depth, p), device_id_type=MESH)
+    for d in others:
+        pl.semaphore_signal(barrier, inc=1, device_id=(d, slab), device_id_type=MESH)
+
     @pl.when(adjoint)
     def _():
         pltpu.make_async_copy(cot_hbm.at[which_field], field, load.at[0]).start()
@@ -171,7 +175,9 @@
         pltpu.make_async_copy(phase_hbm, phase, load.at[3]),
         pltpu.make_async_copy(trans_hbm, tbuf.at[depth], load.at[4]),
     ]
-    mat_loads = [pltpu.make_async_copy(mats_hbm.at[k], mats.at[k], load_mat.at[k]) for k in range(6)]
+    mat_loads = [pltpu.make_async_copy(mats_hbm.at[k], mats.at[k], load_mat.at[k]) for k in range(4)]
+    mat_loads.append(pltpu.make_async_copy(half_fwd_hbm, half_fwd, load_mat.at[4]))
+    mat_loads.append(pltpu.make_async_copy(half_inv_hbm, half_inv, load_mat.at[5]))
     loads[0].start()
     mat_loads[0].start()
     for copy in loads[1:] + mat_loads[1:]:
@@ -182,13 +188,8 @@
         for m in range(2):
             pltpu.make_async_copy(inc_hbm.at[m], results.at[2 + m], load.at[5 + m]).start()
 
-    barrier = pltpu.get_barrier_semaphore()
-    for p in partners:
-        pl.semaphore_signal(barrier, inc=1, device_id=(depth, p), device_id_type=MESH)
-    for d in others:
-        pl.semaphore_signal(barrier, inc=1, device_id=(d, slab), device_id_type=MESH)
-
     zbuf[144:, :] = jnp.zeros((112, 512), F32)
+    hbuf[0] = jnp.zeros((192, 256), F32)
     orient = jnp.where(forward, 1.0, -1.0).astype(F32)
 
     def t_copy(d):
@@ -211,21 +212,23 @@
         cur[:ROWS] = (fr * tr - fi * ti).astype(BF16).astype(F32)
         cur[ROWS:] = (fr * ti + fi * tr).astype(BF16).astype(F32)
 
+    def send_to(which, plane, p, sent, sent_rest, received, received_rest):
+        pltpu.make_async_remote_copy(
+            src_ref=sent.at[p], dst_ref=received.at[slab], send_sem=a2a_send.at[which, 0],
+            recv_sem=a2a_recv.at[which, 0], device_id=(plane, p), device_id_type=MESH).start()
+        pltpu.make_async_remote_copy(
+            src_ref=sent_rest.at[p], dst_ref=received_rest.at[slab], send_sem=a2a_send.at[which, 1],
+            recv_sem=a2a_recv.at[which, 1], device_id=(plane, p), device_id_type=MESH).start()
+
     def exchange(which, sent, sent_rest, received, received_rest):
         for p in partners:
-            pltpu.make_async_remote_copy(
-                src_ref=sent.at[p], dst_ref=received.at[slab], send_sem=a2a_send.at[which, 0],
-                recv_sem=a2a_recv.at[which, 0], device_id=(depth, p), device_id_type=MESH).start()
-            pltpu.make_async_remote_copy(
-                src_ref=sent_rest.at[p], dst_ref=received_rest.at[slab], send_sem=a2a_send.at[which, 1],
-                recv_sem=a2a_recv.at[which, 1], device_id=(depth, p), device_id_type=MESH).start()
+            send_to(which, depth, p, sent, sent_rest, received, received_rest)
         received[slab] = sent[slab]
         received_rest[slab] = sent_rest[slab]
 
-    def finish(which, sent, sent_rest, received, received_rest):
-        for k, ref, sem in ((0, sent, a2a_send), (1, sent_rest, a2a_send),
-                            (0, received, a2a_recv), (1, received_rest, a2a_recv)):
-            part = ref.at[pl.ds(0, SLABS - 1)]
+    def wait_all(sem, which, count, main, rest):
+        for k, ref in enumerate((main, rest)):
+            part = ref.at[pl.ds(0, count)]
             pltpu.make_async_copy(part, part, sem.at[which, k]).wait()
 
     def stage_a():
@@ -241,40 +244,43 @@
         pack(dot(mats[0], zbuf[...].astype(BF16), ((1,), (1,))), send1, send1r, fold)
 
     def make_filter():
-        lane = lax.broadcasted_iota(jnp.int32, (SLABS, 128), 1)
-        pbuf[...] = jnp.zeros_like(pbuf)
-        for chunk, count in ((0, 16), (1, 8)):
-            acc = [jnp.zeros((SLABS, 128), F32) for _ in range(KEEP)]
-            for i in range(count):
-                if i % 2 == 0:
-                    lo = 64 * (16 * chunk + i)
-                    pbuf[:ROWS] = phase[:, lo : lo + 128]
-                    turned = pbuf[...].T
-                block = turned[64 * (i % 2) : 64 * (i % 2) + 64]
-                inside = (lane >= 8 * i) & (lane < 8 * i + SMALL)
-                for k in range(KEEP):
-                    moved = pltpu.roll(block, (8 * i - SMALL * k) % 128, 1)
-                    acc[k] = jnp.where(inside, moved, acc[k])
-            for k in range(KEEP):
-                hbuf[0, 64 * k : 64 * k + 64, 128 * chunk : 128 * chunk + 128] = jnp.cos(acc[k])
-                hbuf[1, 64 * k : 64 * k + 64, 128 * chunk : 128 * chunk + 128] = jnp.sin(acc[k]) * orient
+        for p in range(ROWS):
+            lo = 128 * (p // 2)
+            for chunk in range(2):
+                low = phase[12 * chunk : 12 * chunk + SMALL, lo : lo + 128]
+                high = phase[12 * chunk + SMALL : 12 * chunk + 12, lo : lo + 128]
+                if p % 2 == 0:
+                    high = pltpu.roll(high, 64, 1)
+                else:
+                    low = pltpu.roll(low, 64, 1)
+                lane = lax.broadcasted_iota(jnp.int32, (SMALL, 128), 1)
+                angles = jnp.where(lane < 64, low, high)
+                hbuf[0, 8 * p : 8 * p + SMALL, 128 * chunk : 128 * chunk + 128] = angles
+        angles = hbuf[0]
+        hbuf[0] = jnp.cos(angles)
+        hbuf[1] = jnp.sin(angles) * orient
 
     def stage_b():
-        y = dot(mats[1], unpack(recv1, recv1r, fold))
-        c, s = col_tw[0][None], col_tw[1][None]
-        yr, yi = y[:256].reshape(KEEP, 64, 256), y[256:].reshape(KEEP, 64, 256)
-        z = jnp.concatenate([(yr * c + yi * s).reshape(256, 256), (yi * c - yr * s).reshape(256, 256)], axis=1)
-        y = dot(z.astype(BF16), mats[2])
-        yr, yi, hr, hi = y[:, :256], y[:, 256:], hbuf[0], hbuf[1]
-        z = jnp.concatenate([yr * hr - yi * hi, yi * hr + yr * hi], axis=1)
-        y = dot(z.astype(BF16), mats[3])
-        yr, yi = y[:, :256].reshape(KEEP, 64, 256), y[:, 256:].reshape(KEEP, 64, 256)
+        y = dot(unpack(recv1, recv1r, fold)[:, :144], mats[1], ((0,), (0,)))
+        c, s = col_tw[0], col_tw[1]
+        parts = [[], []]
+        for j in range(SMALL):
+            yr, yi = y[ROWS * j : ROWS * j + ROWS, :256], y[ROWS * j : ROWS * j + ROWS, 256:]
+            parts[0].append(yr * c + yi * s)
+            parts[1].append(yi * c - yr * s)
+        y = dot(half_fwd[...], jnp.concatenate(parts[0] + parts[1], axis=0).astype(BF16))
+        yr, yi, hr, hi = y[:192], y[192:], hbuf[0], hbuf[1]
+        z = jnp.concatenate([yr * hr - yi * hi, yi * hr + yr * hi], axis=0)
+        y = dot(half_inv[...], z.astype(BF16))
         c, s = c * (1.0 / N), s * (1.0 / N)
-        z = jnp.concatenate([(yr * c - yi * s).reshape(256, 256), (yi * c + yr * s).reshape(256, 256)], axis=0)
-        pack(dot(mats[4], z.astype(BF16)), send2, send2r, fold)
-
-    def stage_c(turn):
-        zbuf_c = dot(unpack(recv2, recv2r, fold), mats[5], ((0,), (0,)))
+        for j in range(SMALL):
+            yr, yi = y[ROWS * j : ROWS * j + ROWS], y[144 + ROWS * j : 144 + ROWS * j + ROWS]
+            zbuf[ROWS * j : ROWS * j + ROWS, :256] = yr * c - yi * s
+            zbuf[ROWS * j : ROWS * j + ROWS, 256:] = yi * c + yr * s
+        pack(dot(mats[2], zbuf[...].astype(BF16), ((1,), (1,))), send2, send2r, fold)
+
+    def stage_c(main, rest, target, index):
+        zbuf_c = dot(unpack(main, rest, fold)[:, :144], mats[3], ((0,), (0,)))
         for half in range(2):
             lo = 128 * half
             x = []
@@ -286,7 +292,7 @@
                 x.append((zr * c - zi * s, zi * c + zr * s))
             for a, (vr, vi) in enumerate(dft_six(x, -1.0)):
                 both = jnp.concatenate([vr, vi], axis=0)
-                outgoing[turn, :, BIG * a + lo : BIG * a + lo + 128] = both.astype(BF16)
+                target[index, :, BIG * a + lo : BIG * a + lo + 128] = both.astype(BF16)
 
     def r_copy(turn, target):
         return pltpu.make_async_remote_copy(
@@ -324,41 +330,63 @@
     for copy in loads[1:2] + mat_loads[1:]:
         copy.wait()
 
+    first = send1, send1r, recv1, recv1r
+    second = send2, send2r, recv2, recv2r
+    last = DEPTH - 1
+    most = SLABS - 1
+
     @pl.loop(0, DEPTH)
     def _(turn):
-        @pl.when(adjoint | (turn < DEPTH - 1))
+        @pl.when(adjoint | (turn < last))
         def _():
-            first = send1, send1r, recv1, recv1r
-            second = send2, send2r, recv2, recv2r
             exchange(0, *first)
-            finish(0, *first)
+            wait_all(a2a_recv, 0, most, recv1, recv1r)
+
+            @pl.when(turn > 0)
+            def _():
+                wait_all(a2a_send, 1, most, send2, send2r)
+
             stage_b()
-            exchange(1, *second)
-            finish(1, *second)
-            stage_c(turn)
-            target = target_of(turn)
-
-            @pl.when(target != depth)
+            direct = (depth == 1) & (turn == last)
+
+            @pl.when(direct)
             def _():
-                r_copy(turn, target).start()
-
-            @pl.when(target == depth)
+                pltpu.make_async_copy(field, results.at[0], r_recv.at[0]).wait()
+                for p in partners + [slab]:
+                    send_to(2, 0, p, send2, send2r, recv3, recv3r)
+                wait_all(a2a_send, 0, most, send1, send1r)
+
+            @pl.when(jnp.logical_not(direct))
             def _():
-                results[depth] = outgoing[turn]
-
-            @pl.when(jnp.where(forward, turn < DEPTH - 2, turn < DEPTH - 1))
-            def _():
-                t_arrived(target)
-                multiply(outgoing[turn], target)
-                stage_a()
+                exchange(1, *second)
+                wait_all(a2a_recv, 1, most, recv2, recv2r)
+                wait_all(a2a_send, 0, most, send1, send1r)
+                stage_c(recv2, recv2r, outgoing, turn)
+                target = target_of(turn)
+
+                @pl.when(target != depth)
+                def _():
+                    r_copy(turn, target).start()
+
+                @pl.when(target == depth)
+                def _():
+                    results[depth] = outgoing[turn]
+
+                @pl.when(jnp.where(forward, turn < last - 1, turn < last))
+                def _():
+                    t_arrived(target)
+                    multiply(outgoing[turn], target)
+                    stage_a()
 
     @pl.when(depth == 0)
     def _():
         for m in range(2):
             pltpu.make_async_copy(inc_hbm.at[m], results.at[2 + m], load.at[5 + m]).wait()
-
-    for slot in range(DEPTH):
-        @pl.when((depth != slot) & ((slot < 2) | (depth >= 1)))
+        wait_all(a2a_recv, 2, SLABS, recv3, recv3r)
+        stage_c(recv3, recv3r, results, 1)
+
+    for slot, needed in ((0, depth >= 2), (1, depth >= 2), (2, (depth == 1) | (depth == 3)), (3, (depth == 1) | (depth == 2))):
+        @pl.when(needed)
         def _(slot=slot):
             pltpu.make_async_copy(field, results.at[slot], r_recv.at[slot]).wait()
 
@@ -378,16 +406,24 @@
         def _(d=d):
             t_copy(d).wait_send()
 
-    for turn in range(DEPTH):
+    for turn in range(last):
         target = target_of(turn)
 
-        @pl.when((target != depth) & (adjoint | (turn < DEPTH - 1)))
+        @pl.when(target != depth)
         def _(turn=turn, target=target):
             r_copy(turn, target).wait_send()
 
+    @pl.when(depth == 1)
+    def _():
+        wait_all(a2a_send, 2, SLABS, send2, send2r)
+
+    @pl.when(depth != 1)
+    def _():
+        wait_all(a2a_send, 1, most, send2, send2r)
+
 
 def on_device(incident, transmission, prop_phase, cotangent):
-    mats, row_tw, col_tw = (jnp.asarray(t) for t in make_tables())
+    mats, half_fwd, half_inv, row_tw, col_tw = (jnp.asarray(t) for t in make_tables())
     inc = incident.reshape(2, 2 * ROWS, N)
     trans = transmission.reshape(2 * ROWS, N)
     cot = cotangent.reshape(2, 2 * ROWS, N)
@@ -399,30 +435,31 @@
     grads = pl.pallas_call(
         kernel,
         out_shape=jax.ShapeDtypeStruct(field, F32),
-        in_specs=[hbm] * 7,
+        in_specs=[hbm] * 9,
         out_specs=pl.BlockSpec(memory_space=pltpu.VMEM),
         scratch_shapes=[
             pltpu.VMEM(field, BF16),
             pltpu.VMEM((ROWS, N), F32),
             pltpu.VMEM(mats.shape, BF16),
+            pltpu.VMEM(half_fwd.shape, BF16),
+            pltpu.VMEM(half_inv.shape, BF16),
             pltpu.VMEM(row_tw.shape, F32),
             pltpu.VMEM(col_tw.shape, F32),
             pltpu.VMEM((DEPTH,) + field, BF16),
             pltpu.VMEM(field, F32),
             pltpu.VMEM((256, 512), F32),
             pltpu.VMEM((512, 128), F32),
-            main, rest, main, rest, main, rest, main, rest,
+            main, rest, main, rest, main, rest, main, rest, main, rest,
             pltpu.VMEM((DEPTH,) + field, BF16),
-            pltpu.VMEM((2, 256, 256), F32),
-            pltpu.VMEM((128, 128), F32),
+            pltpu.VMEM((2, 192, 256), F32),
             pltpu.VMEM((DEPTH,) + field, BF16),
-            dma((7,)), dma((6,)), dma((2, 2)), dma((2, 2)),
+            dma((7,)), dma((6,)), dma((3, 2)), dma((3, 2)),
             dma((DEPTH,)), dma((DEPTH,)), dma((DEPTH,)), dma((DEPTH,)),
         ],
         compiler_params=pltpu.CompilerParams(
             collective_id=0, has_side_effects=True, vmem_limit_bytes=62 * 2**20),
         name="chains",
-    )(inc, trans, prop_phase.T, cot, mats, row_tw, col_tw)
+    )(inc, trans, prop_phase.T, cot, mats, half_fwd, half_inv, row_tw, col_tw)
     return grads.reshape(1, 2, ROWS, N)
 
 

time: 85.3 us -> 79.8 us (0.936)
  Pallas kernels: 83.5 us -> 78 us
    pallas_call x1, Pallas kernels: 83.5 us -> 78 us  [on_device(): pl.pallas_call(kernel, out_shape=jax.ShapeDtypeStruct(field, F32), in_spe...]
where the time goes in v3:
time: 79.8 us; the launch traced here: 79.7 us
  Pallas kernels  78 us (98%)
  local copies, waits for them, and re-layouts  1.69 us (2%)
    pallas_call x1, Pallas kernels, on_device(): pl.pallas_call(kernel, out_shape=jax.ShapeDtypeStruct(field, F32), in_spe...  78 us
    unnamed x1, local copies, waits for them, and re-layouts  1.69 us

profile of v3, /device:TPU:1, one launch (start us, length us, event | category | flops | bytes accessed | tf_op | source)
XLA Modules:
  0.0 79.7 jit_solution(14979859521988050742)
XLA Ops:
  0.0 78.0 %chains.1 = f32[48,1536]{1,0:T(8,128)} custom-call(bf16[2,48,1536]{2,1,0:T(8,128)(2,1)} %bitcast.6, bf16[48,1536]{1,0:T(8,128)(2,1)} %bitcast.8, f32[24,1536]{1,0:T(8,128)} %bitcast.9, bf16[2,48,1536]{2,1,0:T(8,128)(2,1)} %bitcast.7, bf16[4,512,512]{2,1,0:T(8,128)(2,1)} %constant.10.clone.mats_hbm, bf16[384,288]{1,0:T(8,128)(2,1)} %constant.11.clone.half_fwd_hbm, ...), custom_call_target="tpu_custom_call" | custom-call | tf_op jit(solution)/shard_map/chains/pallas_call | solution.py:435
  78.0 1.7 %copy.11 = f32[1,2,24,1536]{3,2,1,0:T(8,128)} copy(f32[1,2,24,1536]{3,2,1,0:T(8,128)} %bitcast.5) | data formatting | bytes 589824

commit v4 on v3

--- a/solution.py
+++ b/solution.py
@@ -16,6 +16,7 @@
 SMALL = N // BIG
 KEEP = BIG // SLABS
 DEPTH = 4
+GROUP = SMALL // 2
 MESH = pl.DeviceIdType.MESH
 F32 = jnp.float32
 BF16 = jnp.bfloat16
@@ -36,47 +37,42 @@
     freq = np.arange(BIG)
     samp = np.arange(BIG)
     cos, sin = angle(freq[:, None] * samp[None, :], BIG)
-    full = np.zeros((SLABS, 2, KEEP, 2, BIG))
-    c4, s4 = cos.reshape(SLABS, KEEP, BIG), sin.reshape(SLABS, KEEP, BIG)
-    full[:, 0, :, 0], full[:, 0, :, 1] = c4, s4
-    full[:, 1, :, 0], full[:, 1, :, 1] = -s4, c4
-    row_fwd = full.reshape(512, 512)
-    full = np.zeros((SLABS, 2, KEEP, 2, BIG))
-    full[:, 0, :, 0], full[:, 0, :, 1] = c4, s4
-    full[:, 1, :, 0], full[:, 1, :, 1] = -s4, c4
-    row_inv = full.reshape(512, 512)
+    cos = cos.reshape(SLABS, 2, 2, BIG).transpose(1, 2, 0, 3)
+    sin = sin.reshape(SLABS, 2, 2, BIG).transpose(1, 2, 0, 3)
+    full = np.zeros((2, 2, 2, SLABS, 2, BIG))
+    full[:, 0, :, :, 0], full[:, 0, :, :, 1] = cos, sin
+    full[:, 1, :, :, 0], full[:, 1, :, :, 1] = -sin, cos
+    rows = full.reshape(512, 512)
     m64 = np.arange(SLABS)
     cos, sin = angle(m64[:, None] * m64[None, :], SLABS)
-    full = np.zeros((2, KEEP, SLABS, SLABS, 2, KEEP))
-    back = np.zeros((SLABS, 2, KEEP, 2, KEEP, SLABS))
-    for k in range(KEEP):
-        full[0, k, :, :, 0, k], full[0, k, :, :, 1, k] = cos, sin
-        full[1, k, :, :, 0, k], full[1, k, :, :, 1, k] = -sin, cos
-        back[:, 0, k, 0, k, :], back[:, 0, k, 1, k, :] = cos, -sin
-        back[:, 1, k, 0, k, :], back[:, 1, k, 1, k, :] = sin, cos
-    col_fwd = full.reshape(512, 512)
-    col_inv = back.reshape(512, 512)
-    half_fwd = np.zeros((2, 192, 2, 144))
-    half_inv = np.zeros((2, 144, 2, 192))
+    full = np.zeros((2, 2, SLABS, 2, 2, SLABS))
+    back = np.zeros((2, 2, SLABS, 2, 2, SLABS))
+    for k in range(2):
+        full[0, k, :, 0, k], full[1, k, :, 0, k] = cos, sin
+        full[0, k, :, 1, k], full[1, k, :, 1, k] = -sin, cos
+        back[0, k, :, 0, k], back[0, k, :, 1, k] = cos, -sin
+        back[1, k, :, 0, k], back[1, k, :, 1, k] = sin, cos
+    cols = np.stack([full.reshape(256, 256), back.reshape(256, 256)])
+    half_fwd = np.zeros((2, 96, 2, 72))
+    half_inv = np.zeros((2, 72, 2, 96))
     rho = np.arange(ROWS)
     cos, sin = angle(rho[:, None] * rho[None, :], ROWS)
-    for j in range(SMALL):
+    for j in range(GROUP):
         a = 24 * j + rho[None, :]
-        b = 8 * rho[:, None] + j
+        b = 4 * rho[:, None] + j
         half_fwd[0, b, 0, a], half_fwd[0, b, 1, a] = cos, sin
         half_fwd[1, b, 0, a], half_fwd[1, b, 1, a] = -sin, cos
         half_inv[0, a, 0, b], half_inv[0, a, 1, b] = cos, -sin
         half_inv[1, a, 0, b], half_inv[1, a, 1, b] = sin, cos
-    half_fwd = half_fwd.reshape(384, 288)
-    half_inv = half_inv.reshape(288, 384)
+    half_fwd = half_fwd.reshape(192, 144)
+    half_inv = half_inv.reshape(144, 192)
     cos, sin = angle(np.arange(SMALL)[:, None] * samp[None, :], N)
     row_tw = np.zeros((2, 8, BIG))
     row_tw[0, :SMALL], row_tw[1, :SMALL] = cos, sin
     cos, sin = angle(rho[:, None] * m64[None, :], N)
-    col_tw = np.stack([np.tile(cos, (1, KEEP)), np.tile(sin, (1, KEEP))])
-    mats = np.stack([row_fwd, col_fwd.T, col_inv, row_inv])
+    col_tw = np.stack([np.tile(cos, (1, 2)), np.tile(sin, (1, 2))])
     f32 = lambda a: np.asarray(a, np.float32)
-    return bf(mats), bf(half_fwd), bf(half_inv), f32(row_tw), f32(col_tw)
+    return bf(rows), bf(cols), bf(half_fwd), bf(half_inv), f32(row_tw), f32(col_tw)
 
 
 def dot(a, b, dims=((1,), (0,))):
@@ -104,22 +100,30 @@
     return out
 
 
-def pack(y, main, rest, fold):
-    main[...] = y[:, :128].reshape(SLABS, 8, 128).astype(BF16)
-    fold[...] = y[:, 128:]
-    row = fold[pl.ds(0, SLABS, stride=8), :]
-    for i in range(1, 8):
-        row = row + pltpu.roll(fold[pl.ds(i, SLABS, stride=8), :], 16 * i, 1)
+def pack(y, first, row, fold):
+    for i in range(y.shape[0] // SLABS):
+        block = y[SLABS * i : SLABS * i + SLABS]
+        fold[pl.ds(first + i, SLABS, stride=8), :] = block[:, :128]
+        tail = block[:, 128:]
+        if first + i > 0:
+            tail = pltpu.roll(tail, 16 * (first + i), 1)
+        row = tail if row is None else row + tail
+    return row
+
+
+def finish_pack(row, main, rest, fold):
+    main[...] = fold[...].reshape(SLABS, 8, 128).astype(BF16)
     rest[...] = row.reshape(SLABS, 1, 128)
 
 
 def unpack(main, rest, fold):
+    fold[...] = main[...].astype(F32).reshape(512, 128)
     row = rest[...].reshape(SLABS, 128)
-    fold[pl.ds(0, SLABS, stride=8), :] = row
-    for i in range(1, 8):
-        fold[pl.ds(i, SLABS, stride=8), :] = pltpu.roll(row, 128 - 16 * i, 1)
-    both = [main[...].astype(F32).reshape(512, 128), fold[...]]
-    return jnp.concatenate(both, axis=1).astype(BF16)
+    blocks = []
+    for i in range(8):
+        tail = pltpu.roll(row, 128 - 16 * i, 1) if i else row
+        blocks.append(jnp.concatenate([fold[pl.ds(i, SLABS, stride=8), :], tail], axis=1))
+    return jnp.concatenate(blocks, axis=0).astype(BF16)
 
 
 def hop(a, n):
@@ -138,9 +142,17 @@
     return out + rest[len(plus) :]
 
 
-def kernel(inc_hbm, trans_hbm, phase_hbm, cot_hbm, mats_hbm, half_fwd_hbm, half_inv_hbm, row_tw_hbm,
-           col_tw_hbm, out, field, phase, mats, half_fwd, half_inv, row_tw, col_tw,
-           tbuf, cur, zbuf, fold, send1, send1r, recv1, recv1r, send2, send2r, recv2, recv2r,
+def final_order():
+    slabs = [(y * 16 + z * 2 + c, z) for z in range(8) for y in range(4) for c in range(2)]
+    slabs.sort(key=lambda t: (t[0] != 1, t[1] != 0))
+    head, tail = slabs[:1], slabs[1:]
+    tail.sort(key=lambda t: (t[0] * 29) % 64)
+    return [p for p, _ in head + tail]
+
+
+def kernel(inc_hbm, trans_hbm, phase_hbm, cot_hbm, rows_hbm, cols_hbm, half_fwd_hbm, half_inv_hbm, row_tw_hbm,
+           col_tw_hbm, out, field, phase, rows, cols, half_fwd, half_inv, row_tw, col_tw,
+           tbuf, cur, zbuf, zcol, fold, send1, send1r, recv1, recv1r, send2, send2r, recv2, recv2r,
            recv3, recv3r, results, hbuf, outgoing,
            load, load_mat, a2a_send, a2a_recv, t_send, t_recv, r_send, r_recv):
     depth = lax.axis_index("depth")
@@ -175,9 +187,12 @@
         pltpu.make_async_copy(phase_hbm, phase, load.at[3]),
         pltpu.make_async_copy(trans_hbm, tbuf.at[depth], load.at[4]),
     ]
-    mat_loads = [pltpu.make_async_copy(mats_hbm.at[k], mats.at[k], load_mat.at[k]) for k in range(4)]
-    mat_loads.append(pltpu.make_async_copy(half_fwd_hbm, half_fwd, load_mat.at[4]))
-    mat_loads.append(pltpu.make_async_copy(half_inv_hbm, half_inv, load_mat.at[5]))
+    mat_loads = [
+        pltpu.make_async_copy(rows_hbm, rows, load_mat.at[0]),
+        pltpu.make_async_copy(cols_hbm, cols, load_mat.at[1]),
+        pltpu.make_async_copy(half_fwd_hbm, half_fwd, load_mat.at[2]),
+        pltpu.make_async_copy(half_inv_hbm, half_inv, load_mat.at[3]),
+    ]
     loads[0].start()
     mat_loads[0].start()
     for copy in loads[1:] + mat_loads[1:]:
@@ -189,7 +204,8 @@
             pltpu.make_async_copy(inc_hbm.at[m], results.at[2 + m], load.at[5 + m]).start()
 
     zbuf[144:, :] = jnp.zeros((112, 512), F32)
-    hbuf[0] = jnp.zeros((192, 256), F32)
+    zcol[:, 144:, :] = jnp.zeros((2, 112, 256), F32)
+    hbuf[0] = jnp.zeros((2, 96, 256), F32)
     orient = jnp.where(forward, 1.0, -1.0).astype(F32)
 
     def t_copy(d):
@@ -241,46 +257,66 @@
                 s = row_tw[1, j : j + 1, lo : lo + 128]
                 zbuf[ROWS * j : ROWS * j + ROWS, lo : lo + 128] = zr * c + zi * s
                 zbuf[ROWS * j : ROWS * j + ROWS, BIG + lo : BIG + lo + 128] = zi * c - zr * s
-        pack(dot(mats[0], zbuf[...].astype(BF16), ((1,), (1,))), send1, send1r, fold)
+        row = pack(dot(rows[...], zbuf[...].astype(BF16), ((1,), (1,))), 0, None, fold)
+        finish_pack(row, send1, send1r, fold)
 
     def make_filter():
+        lane = lax.broadcasted_iota(jnp.int32, (SMALL, 128), 1)
         for p in range(ROWS):
             lo = 128 * (p // 2)
-            for chunk in range(2):
-                low = phase[12 * chunk : 12 * chunk + SMALL, lo : lo + 128]
-                high = phase[12 * chunk + SMALL : 12 * chunk + 12, lo : lo + 128]
+            for h in range(2):
+                low = phase[12 * h : 12 * h + SMALL, lo : lo + 128]
+                high = phase[12 * h + SMALL : 12 * h + 12, lo : lo + 128]
                 if p % 2 == 0:
                     high = pltpu.roll(high, 64, 1)
                 else:
                     low = pltpu.roll(low, 64, 1)
-                lane = lax.broadcasted_iota(jnp.int32, (SMALL, 128), 1)
                 angles = jnp.where(lane < 64, low, high)
-                hbuf[0, 8 * p : 8 * p + SMALL, 128 * chunk : 128 * chunk + 128] = angles
+                for g in range(2):
+                    hbuf[0, h, 4 * p : 4 * p + GROUP, 128 * g : 128 * g + 128] = (
+                        angles[GROUP * g : GROUP * g + GROUP])
         angles = hbuf[0]
         hbuf[0] = jnp.cos(angles)
         hbuf[1] = jnp.sin(angles) * orient
 
     def stage_b():
-        y = dot(unpack(recv1, recv1r, fold)[:, :144], mats[1], ((0,), (0,)))
+        x = unpack(recv1, recv1r, fold)[:, :144]
         c, s = col_tw[0], col_tw[1]
-        parts = [[], []]
-        for j in range(SMALL):
-            yr, yi = y[ROWS * j : ROWS * j + ROWS, :256], y[ROWS * j : ROWS * j + ROWS, 256:]
-            parts[0].append(yr * c + yi * s)
-            parts[1].append(yi * c - yr * s)
-        y = dot(half_fwd[...], jnp.concatenate(parts[0] + parts[1], axis=0).astype(BF16))
-        yr, yi, hr, hi = y[:192], y[192:], hbuf[0], hbuf[1]
-        z = jnp.concatenate([yr * hr - yi * hi, yi * hr + yr * hi], axis=0)
-        y = dot(half_inv[...], z.astype(BF16))
-        c, s = c * (1.0 / N), s * (1.0 / N)
-        for j in range(SMALL):
-            yr, yi = y[ROWS * j : ROWS * j + ROWS], y[144 + ROWS * j : 144 + ROWS * j + ROWS]
-            zbuf[ROWS * j : ROWS * j + ROWS, :256] = yr * c - yi * s
-            zbuf[ROWS * j : ROWS * j + ROWS, 256:] = yi * c + yr * s
-        pack(dot(mats[2], zbuf[...].astype(BF16), ((1,), (1,))), send2, send2r, fold)
+        cs, ss = c * (1.0 / N), s * (1.0 / N)
+        halves = [dot(x[256 * h : 256 * h + 256], cols[0], ((0,), (0,))) for h in range(2)]
+        for h, y in enumerate(halves):
+            parts = [[], []]
+            for i in range(GROUP):
+                wide = [[], []]
+                for g in range(2):
+                    j = GROUP * g + i
+                    yr, yi = y[ROWS * j : ROWS * j + ROWS, :128], y[ROWS * j : ROWS * j + ROWS, 128:]
+                    wide[0].append(yr * c + yi * s)
+                    wide[1].append(yi * c - yr * s)
+                parts[0].append(jnp.concatenate(wide[0], axis=1))
+                parts[1].append(jnp.concatenate(wide[1], axis=1))
+            halves[h] = jnp.concatenate(parts[0] + parts[1], axis=0).astype(BF16)
+        halves = [dot(half_fwd[...], x) for x in halves]
+        for h, x in enumerate(halves):
+            xr, xi, hr, hi = x[:96], x[96:], hbuf[0, h], hbuf[1, h]
+            halves[h] = jnp.concatenate([xr * hr - xi * hi, xi * hr + xr * hi], axis=0).astype(BF16)
+        halves = [dot(half_inv[...], x) for x in halves]
+        for h, x in enumerate(halves):
+            for i in range(GROUP):
+                for g in range(2):
+                    j = GROUP * g + i
+                    xr = x[ROWS * i : ROWS * i + ROWS, 128 * g : 128 * g + 128]
+                    xi = x[72 + ROWS * i : 72 + ROWS * i + ROWS, 128 * g : 128 * g + 128]
+                    zcol[h, ROWS * j : ROWS * j + ROWS, :128] = xr * cs - xi * ss
+                    zcol[h, ROWS * j : ROWS * j + ROWS, 128:] = xi * cs + xr * ss
+        halves = [dot(cols[1], zcol[h].astype(BF16), ((1,), (1,))) for h in range(2)]
+        row = None
+        for h, y in enumerate(halves):
+            row = pack(y, 4 * h, row, fold)
+        finish_pack(row, send2, send2r, fold)
 
     def stage_c(main, rest, target, index):
-        zbuf_c = dot(unpack(main, rest, fold)[:, :144], mats[3], ((0,), (0,)))
+        zbuf_c = dot(unpack(main, rest, fold)[:, :144], rows[...], ((0,), (0,)))
         for half in range(2):
             lo = 128 * half
             x = []
@@ -352,13 +388,25 @@
             @pl.when(direct)
             def _():
                 pltpu.make_async_copy(field, results.at[0], r_recv.at[0]).wait()
-                for p in partners + [slab]:
+                for p in final_order():
                     send_to(2, 0, p, send2, send2r, recv3, recv3r)
                 wait_all(a2a_send, 0, most, send1, send1r)
 
             @pl.when(jnp.logical_not(direct))
             def _():
-                exchange(1, *second)
+                @pl.when(turn < last)
+                def _():
+                    exchange(1, *second)
+
+                @pl.when(turn == last)
+                def _():
+                    for p in final_order():
+                        @pl.when(p != slab)
+                        def _(p=p):
+                            send_to(1, 0, p, *second)
+                    recv2[slab] = send2[slab]
+                    recv2r[slab] = send2r[slab]
+
                 wait_all(a2a_recv, 1, most, recv2, recv2r)
                 wait_all(a2a_send, 0, most, send1, send1r)
                 stage_c(recv2, recv2r, outgoing, turn)
@@ -423,7 +471,7 @@
 
 
 def on_device(incident, transmission, prop_phase, cotangent):
-    mats, half_fwd, half_inv, row_tw, col_tw = (jnp.asarray(t) for t in make_tables())
+    rows, cols, half_fwd, half_inv, row_tw, col_tw = (jnp.asarray(t) for t in make_tables())
     inc = incident.reshape(2, 2 * ROWS, N)
     trans = transmission.reshape(2 * ROWS, N)
     cot = cotangent.reshape(2, 2 * ROWS, N)
@@ -435,12 +483,13 @@
     grads = pl.pallas_call(
         kernel,
         out_shape=jax.ShapeDtypeStruct(field, F32),
-        in_specs=[hbm] * 9,
+        in_specs=[hbm] * 10,
         out_specs=pl.BlockSpec(memory_space=pltpu.VMEM),
         scratch_shapes=[
             pltpu.VMEM(field, BF16),
             pltpu.VMEM((ROWS, N), F32),
-            pltpu.VMEM(mats.shape, BF16),
+            pltpu.VMEM(rows.shape, BF16),
+            pltpu.VMEM(cols.shape, BF16),
             pltpu.VMEM(half_fwd.shape, BF16),
             pltpu.VMEM(half_inv.shape, BF16),
             pltpu.VMEM(row_tw.shape, F32),
@@ -448,18 +497,19 @@
             pltpu.VMEM((DEPTH,) + field, BF16),
             pltpu.VMEM(field, F32),
             pltpu.VMEM((256, 512), F32),
+            pltpu.VMEM((2, 256, 256), F32),
             pltpu.VMEM((512, 128), F32),
             main, rest, main, rest, main, rest, main, rest, main, rest,
             pltpu.VMEM((DEPTH,) + field, BF16),
-            pltpu.VMEM((2, 192, 256), F32),
+            pltpu.VMEM((2, 2, 96, 256), F32),
             pltpu.VMEM((DEPTH,) + field, BF16),
-            dma((7,)), dma((6,)), dma((3, 2)), dma((3, 2)),
+            dma((7,)), dma((4,)), dma((3, 2)), dma((3, 2)),
             dma((DEPTH,)), dma((DEPTH,)), dma((DEPTH,)), dma((DEPTH,)),
         ],
         compiler_params=pltpu.CompilerParams(
             collective_id=0, has_side_effects=True, vmem_limit_bytes=62 * 2**20),
         name="chains",
-    )(inc, trans, prop_phase.T, cot, mats, half_fwd, half_inv, row_tw, col_tw)
+    )(inc, trans, prop_phase.T, cot, rows, cols, half_fwd, half_inv, row_tw, col_tw)
     return grads.reshape(1, 2, ROWS, N)
 
 

time: 79.8 us -> 77.1 us (0.966)
  Pallas kernels: 78 us -> 74.6 us
    pallas_call x1, Pallas kernels: 78 us -> 74.6 us  [on_device(): pl.pallas_call(kernel, out_shape=jax.ShapeDtypeStruct(field, F32), in_spe...]
where the time goes in v4:
time: 77.1 us; the launch traced here: 76.3 us
  Pallas kernels  74.6 us (97%)
  local copies, waits for them, and re-layouts  1.69 us (2%)
    pallas_call x1, Pallas kernels, on_device(): pl.pallas_call(kernel, out_shape=jax.ShapeDtypeStruct(field, F32), in_spe...  74.6 us
    unnamed x1, local copies, waits for them, and re-layouts  1.69 us

profile of v4, /device:TPU:1, one launch (start us, length us, event | category | flops | bytes accessed | tf_op | source)
XLA Modules:
  0.0 76.3 jit_solution(1849101432271166260)
XLA Ops:
  0.0 74.6 %chains.1 = f32[48,1536]{1,0:T(8,128)} custom-call(bf16[2,48,1536]{2,1,0:T(8,128)(2,1)} %bitcast.6, bf16[48,1536]{1,0:T(8,128)(2,1)} %bitcast.8, f32[24,1536]{1,0:T(8,128)} %bitcast.9, bf16[2,48,1536]{2,1,0:T(8,128)(2,1)} %bitcast.7, bf16[512,512]{1,0:T(8,128)(2,1)} %constant.12.clone.rows_hbm, bf16[2,256,256]{2,1,0:T(8,128)(2,1)} %constant.13.clone.cols_hbm, ...), custom_call_target="tpu_custom_call" | custom-call | tf_op jit(solution)/shard_map/chains/pallas_call | solution.py:483
  74.6 1.7 %copy.12 = f32[1,2,24,1536]{3,2,1,0:T(8,128)} copy(f32[1,2,24,1536]{3,2,1,0:T(8,128)} %bitcast.5) | data formatting | bytes 589824

commit v5 on v4

--- a/solution.py
+++ b/solution.py
@@ -17,6 +17,7 @@
 KEEP = BIG // SLABS
 DEPTH = 4
 GROUP = SMALL // 2
+EARLY = (1, 2, 17, 4, 3, 19, 33, 48, 35, 16)
 MESH = pl.DeviceIdType.MESH
 F32 = jnp.float32
 BF16 = jnp.bfloat16
@@ -132,22 +133,13 @@
 
 def slab_order():
     offs = [(y, z, c) for y in range(4) for z in range(8) for c in range(2)][1:]
-    offs.sort(key=lambda t: (-(hop(t[0], 4) + hop(t[1], 8)), t[2], t[1], t[0]))
-    plus = [t for t in offs if 0 < t[1] < 4]
-    minus = [t for t in offs if t[1] > 4]
-    rest = [t for t in offs if t[1] in (0, 4)]
-    out = []
-    for i in range(len(plus)):
-        out += [plus[i], minus[i]] + rest[i : i + 1]
-    return out + rest[len(plus) :]
+    offs.sort(key=lambda t: -(1.5 * hop(t[0], 4) + hop(t[1], 8) + 1.2 * t[2]))
+    return offs
 
 
 def final_order():
-    slabs = [(y * 16 + z * 2 + c, z) for z in range(8) for y in range(4) for c in range(2)]
-    slabs.sort(key=lambda t: (t[0] != 1, t[1] != 0))
-    head, tail = slabs[:1], slabs[1:]
-    tail.sort(key=lambda t: (t[0] * 29) % 64)
-    return [p for p, _ in head + tail]
+    tail = sorted((p for p in range(SLABS) if p not in EARLY), key=lambda p: (p * 29) % SLABS)
+    return list(EARLY) + tail
 
 
 def kernel(inc_hbm, trans_hbm, phase_hbm, cot_hbm, rows_hbm, cols_hbm, half_fwd_hbm, half_inv_hbm, row_tw_hbm,
@@ -315,7 +307,28 @@
             row = pack(y, 4 * h, row, fold)
         finish_pack(row, send2, send2r, fold)
 
-    def stage_c(main, rest, target, index):
+    def store(target, index):
+        def put(a, lo, vr, vi):
+            both = jnp.concatenate([vr, vi], axis=0)
+            target[index, :, BIG * a + lo : BIG * a + lo + 128] = both.astype(BF16)
+
+        return put
+
+    def add_product(m):
+        def put(a, lo, vr, vi):
+            at = pl.ds(BIG * a + lo, 128)
+            u = results[2 + m, :, at].astype(F32)
+            ur, ui = u[:ROWS], u[ROWS:]
+            pr, pi = vr.astype(BF16).astype(F32), vi.astype(BF16).astype(F32)
+            gr, gi = ur * pr + ui * pi, ur * pi - ui * pr
+            if m > 0:
+                gr, gi = out[:ROWS, at] + gr, out[ROWS:, at] + gi
+            out[:ROWS, at] = gr
+            out[ROWS:, at] = gi
+
+        return put
+
+    def stage_c(main, rest, put):
         zbuf_c = dot(unpack(main, rest, fold)[:, :144], rows[...], ((0,), (0,)))
         for half in range(2):
             lo = 128 * half
@@ -327,8 +340,7 @@
                 zi = zbuf_c[ROWS * j : ROWS * j + ROWS, BIG + lo : BIG + lo + 128]
                 x.append((zr * c - zi * s, zi * c + zr * s))
             for a, (vr, vi) in enumerate(dft_six(x, -1.0)):
-                both = jnp.concatenate([vr, vi], axis=0)
-                target[index, :, BIG * a + lo : BIG * a + lo + 128] = both.astype(BF16)
+                put(a, lo, vr, vi)
 
     def r_copy(turn, target):
         return pltpu.make_async_remote_copy(
@@ -407,16 +419,19 @@
                     recv2[slab] = send2[slab]
                     recv2r[slab] = send2r[slab]
 
+                target = target_of(turn)
                 wait_all(a2a_recv, 1, most, recv2, recv2r)
                 wait_all(a2a_send, 0, most, send1, send1r)
-                stage_c(recv2, recv2r, outgoing, turn)
-                target = target_of(turn)
+
+                @pl.when(turn < last)
+                def _():
+                    stage_c(recv2, recv2r, store(outgoing, turn))
 
                 @pl.when(target != depth)
                 def _():
                     r_copy(turn, target).start()
 
-                @pl.when(target == depth)
+                @pl.when((target == depth) & (turn < last))
                 def _():
                     results[depth] = outgoing[turn]
 
@@ -430,24 +445,27 @@
     def _():
         for m in range(2):
             pltpu.make_async_copy(inc_hbm.at[m], results.at[2 + m], load.at[5 + m]).wait()
+        stage_c(recv2, recv2r, add_product(0))
         wait_all(a2a_recv, 2, SLABS, recv3, recv3r)
-        stage_c(recv3, recv3r, results, 1)
+        stage_c(recv3, recv3r, add_product(1))
 
     for slot, needed in ((0, depth >= 2), (1, depth >= 2), (2, (depth == 1) | (depth == 3)), (3, (depth == 1) | (depth == 2))):
         @pl.when(needed)
         def _(slot=slot):
             pltpu.make_async_copy(field, results.at[slot], r_recv.at[slot]).wait()
 
-    gr = jnp.zeros((ROWS, N), F32)
-    gi = jnp.zeros((ROWS, N), F32)
-    for m in range(2):
-        u = results[2 + m].astype(F32)
-        p = results[m].astype(F32)
-        ur, ui, pr, pi = u[:ROWS], u[ROWS:], p[:ROWS], p[ROWS:]
-        gr = gr + (ur * pr + ui * pi)
-        gi = gi + (ur * pi - ui * pr)
-    out[:ROWS] = gr
-    out[ROWS:] = gi
+    @pl.when(depth > 0)
+    def _():
+        gr = jnp.zeros((ROWS, N), F32)
+        gi = jnp.zeros((ROWS, N), F32)
+        for m in range(2):
+            u = results[2 + m].astype(F32)
+            p = results[m].astype(F32)
+            ur, ui, pr, pi = u[:ROWS], u[ROWS:], p[:ROWS], p[ROWS:]
+            gr = gr + (ur * pr + ui * pi)
+            gi = gi + (ur * pi - ui * pr)
+        out[:ROWS] = gr
+        out[ROWS:] = gi
 
     for d in others:
         @pl.when(t_needed(depth, d))

time: 77.1 us -> 75 us (0.973)
  Pallas kernels: 74.6 us -> 73.2 us
    pallas_call x1, Pallas kernels: 74.6 us -> 73.2 us  [on_device(): pl.pallas_call(kernel, out_shape=jax.ShapeDtypeStruct(field, F32), in_spe...]
where the time goes in v5:
time: 75 us; the launch traced here: 74.9 us
  Pallas kernels  73.2 us (98%)
  local copies, waits for them, and re-layouts  1.69 us (2%)
    pallas_call x1, Pallas kernels, on_device(): pl.pallas_call(kernel, out_shape=jax.ShapeDtypeStruct(field, F32), in_spe...  73.2 us
    unnamed x1, local copies, waits for them, and re-layouts  1.69 us

profile of v5, /device:TPU:1, one launch (start us, length us, event | category | flops | bytes accessed | tf_op | source)
XLA Modules:
  0.0 74.9 jit_solution(134941956206422281)
XLA Ops:
  0.0 73.2 %chains.1 = f32[48,1536]{1,0:T(8,128)} custom-call(bf16[2,48,1536]{2,1,0:T(8,128)(2,1)} %bitcast.6, bf16[48,1536]{1,0:T(8,128)(2,1)} %bitcast.8, f32[24,1536]{1,0:T(8,128)} %bitcast.9, bf16[2,48,1536]{2,1,0:T(8,128)(2,1)} %bitcast.7, bf16[512,512]{1,0:T(8,128)(2,1)} %constant.12.clone.rows_hbm, bf16[2,256,256]{2,1,0:T(8,128)(2,1)} %constant.13.clone.cols_hbm, ...), custom_call_target="tpu_custom_call" | custom-call | tf_op jit(solution)/shard_map/chains/pallas_call | solution.py:501
  73.2 1.7 %copy.12 = f32[1,2,24,1536]{3,2,1,0:T(8,128)} copy(f32[1,2,24,1536]{3,2,1,0:T(8,128)} %bitcast.5) | data formatting | bytes 589824

commit v6 on v5

--- a/solution.py
+++ b/solution.py
@@ -17,7 +17,7 @@
 KEEP = BIG // SLABS
 DEPTH = 4
 GROUP = SMALL // 2
-EARLY = (1, 2, 17, 4, 3, 19, 33, 48, 35, 16)
+EARLY = (0, 1, 8, 2, 9)
 MESH = pl.DeviceIdType.MESH
 F32 = jnp.float32
 BF16 = jnp.bfloat16
@@ -137,9 +137,10 @@
     return offs
 
 
-def final_order():
-    tail = sorted((p for p in range(SLABS) if p not in EARLY), key=lambda p: (p * 29) % SLABS)
-    return list(EARLY) + tail
+def final_order(core):
+    early = [2 * q + c for q in EARLY for c in (1, 0)]
+    late = sorted((q for q in range(SLABS // 2) if q not in EARLY), key=lambda q: (q * 13) % 32)
+    return early + [2 * q + 1 - core for q in late] + [2 * q + core for q in late]
 
 
 def kernel(inc_hbm, trans_hbm, phase_hbm, cot_hbm, rows_hbm, cols_hbm, half_fwd_hbm, half_inv_hbm, row_tw_hbm,
@@ -400,7 +401,7 @@
             @pl.when(direct)
             def _():
                 pltpu.make_async_copy(field, results.at[0], r_recv.at[0]).wait()
-                for p in final_order():
+                for p in final_order(c0):
                     send_to(2, 0, p, send2, send2r, recv3, recv3r)
                 wait_all(a2a_send, 0, most, send1, send1r)
 
@@ -412,7 +413,7 @@
 
                 @pl.when(turn == last)
                 def _():
-                    for p in final_order():
+                    for p in final_order(c0):
                         @pl.when(p != slab)
                         def _(p=p):
                             send_to(1, 0, p, *second)

time: 75 us -> 74.8 us (level)
  no operation moved by 1% of the time
where the time goes in v6:
time: 74.8 us; the launch traced here: 74.7 us
  Pallas kernels  73 us (98%)
  local copies, waits for them, and re-layouts  1.69 us (2%)
    pallas_call x1, Pallas kernels, on_device(): pl.pallas_call(kernel, out_shape=jax.ShapeDtypeStruct(field, F32), in_spe...  73 us
    unnamed x1, local copies, waits for them, and re-layouts  1.69 us

profile of v6, /device:TPU:1, one launch (start us, length us, event | category | flops | bytes accessed | tf_op | source)
XLA Modules:
  0.0 74.7 jit_solution(6899310432711183456)
XLA Ops:
  0.0 73.0 %chains.1 = f32[48,1536]{1,0:T(8,128)} custom-call(bf16[2,48,1536]{2,1,0:T(8,128)(2,1)} %bitcast.6, bf16[48,1536]{1,0:T(8,128)(2,1)} %bitcast.8, f32[24,1536]{1,0:T(8,128)} %bitcast.9, bf16[2,48,1536]{2,1,0:T(8,128)(2,1)} %bitcast.7, bf16[512,512]{1,0:T(8,128)(2,1)} %constant.12.clone.rows_hbm, bf16[2,256,256]{2,1,0:T(8,128)(2,1)} %constant.13.clone.cols_hbm, ...), custom_call_target="tpu_custom_call" | custom-call | tf_op jit(solution)/shard_map/chains/pallas_call | solution.py:502
  73.0 1.7 %copy.12 = f32[1,2,24,1536]{3,2,1,0:T(8,128)} copy(f32[1,2,24,1536]{3,2,1,0:T(8,128)} %bitcast.5) | data formatting | bytes 589824
